TPU v7x, 128 devices: a whole 4x4x4 slice. The times are simulated.
128 devices in a mesh: segment: 2 (over x_lo), tr: 8 (over x_hi, y), tc: 8 (over z, core).
Axes of the slice: x: 4 (x_hi: 2, x_lo: 2; x = x_hi * 2 + x_lo), y: 4, z: 4, core: 2. Of those that a mesh axis runs over, the one named last changes fastest.
Arguments:
- features: bfloat16 [2, 8192, 1280], P('segment', ('tr', 'tc')), may hold values from -6 to 6
- attn_hidden: bfloat16 [2, 8192, 1280], P('segment', ('tr', 'tc')), may hold values from -0.125 to 0.125
- first_deconv: bfloat16 [1280, 2, 2, 640], P('segment'), may hold values from -0.15625 to 0.15625
- first_bias: float32 [640], replicated, may hold values from -3 to 3
- mid_gain: float32 [640], replicated, may hold values from 0.1 to 1.9
- mid_shift: float32 [640], replicated, may hold values from -1.75 to 1.75
- second_deconv: bfloat16 [640, 2, 2, 320], replicated, may hold values from -0.25 to 0.25
- second_bias: float32 [320], replicated, may hold values from -3 to 3
- half_deconv: bfloat16 [1280, 2, 2, 640], P('segment'), may hold values from -0.15625 to 0.15625
- half_bias: float32 [640], replicated, may hold values from -3 to 3
- lateral_four: bfloat16 [320, 256], replicated, may hold values from -0.3125 to 0.3125
- lateral_eight: bfloat16 [640, 256], replicated, may hold values from -0.25 to 0.25
- lateral_sixteen: bfloat16 [1280, 256], replicated, may hold values from -0.15625 to 0.15625
- lateral_coarse: bfloat16 [1280, 256], replicated, may hold values from -0.15625 to 0.15625
- output_conv: bfloat16 [4, 3, 3, 256, 256], replicated, may hold values from -0.125 to 0.125
- level_gain: float32 [4, 2, 256], replicated, may hold values from 0.1 to 1.9
- level_shift: float32 [4, 2, 256], replicated, may hold values from -1.75 to 1.75
- cotangent_four: bfloat16 [2, 512, 256, 256], P('segment', 'tr', 'tc'), may hold values from -6 to 6
- cotangent_eight: bfloat16 [2, 256, 128, 256], P('segment', 'tr', 'tc'), may hold values from -6 to 6
- cotangent_sixteen: bfloat16 [2, 128, 64, 256], P('segment', 'tr', 'tc'), may hold values from -6 to 6
- cotangent_coarse: bfloat16 [2, 64, 32, 256], P('segment', 'tr', 'tc'), may hold values from -6 to 6
Outputs:
- level_four: bfloat16 [2, 512, 256, 256], P('segment', 'tr', 'tc')
- level_eight: bfloat16 [2, 256, 128, 256], P('segment', 'tr', 'tc')
- level_sixteen: bfloat16 [2, 128, 64, 256], P('segment', 'tr', 'tc')
- level_coarse: bfloat16 [2, 64, 32, 256], P('segment', 'tr', 'tc')
- feature_grad: bfloat16 [2, 8192, 1280], P('segment', ('tr', 'tc'))
- weight_grad: float32 [1280, 1280], P(('segment', 'tr', 'tc'))
All inputs are finite; a program needn't handle non-finite values.
Results may differ from a plain program's by a relative error of at most 0.02.
Values may be sent and summed in bfloat16 or wider, within the bound.
A program may use at most 128 MiB of HBM per device.

v0:
```python
import jax
import jax.numpy as jnp
from jax import lax
from jax.sharding import PartitionSpec as P

EPS = 1e-06


def shifted(array, axis, by):
    devices = lax.axis_size(axis)
    return lax.ppermute(array, axis, [(i, (i + by) % devices) for i in range(devices)])


def with_halo(array, sides, width):
    for axis, dim in sides:
        devices, length = (lax.axis_size(axis), array.shape[dim])
        up = [(i, (i + 1) % devices) for i in range(devices - 1)]
        down = [(j, i) for i, j in up]
        last = lax.slice_in_dim(array, length - width, length, axis=dim)
        leading = lax.slice_in_dim(array, 0, width, axis=dim)
        before = lax.ppermute(last, axis, up)
        after = lax.ppermute(leading, axis, down)
        array = jnp.concatenate([before, array, after], axis=dim)
    return array


def arrange_blocks(flattened, height, breadth, offset):
    outward = flattened.shape[1] // 4
    blocks = flattened.reshape(height, breadth, 2, 2, outward) + offset
    return blocks.transpose(0, 2, 1, 3, 4).reshape(2 * height, 2 * breadth, outward)


def expand_pixels(pixels, weight, offset):
    height, breadth, channels = pixels.shape
    outward = weight.shape[3]
    flattened = jnp.dot(
        pixels.reshape(height * breadth, channels),
        weight.reshape(channels, 4 * outward),
        preferred_element_type=jnp.float32,
    )
    return arrange_blocks(flattened, height, breadth, offset)


def layer_norm(values, factor, offset):
    centre = jnp.mean(values, axis=-1, keepdims=True)
    spread = jnp.mean(jnp.square(values - centre), axis=-1, keepdims=True)
    return (values - centre) * lax.rsqrt(spread + EPS) * factor + offset


def lateral(pixels, weight, factor, offset):
    height, breadth, channels = pixels.shape
    projected = jnp.dot(
        pixels.reshape(height * breadth, channels), weight, preferred_element_type=jnp.float32
    )
    return layer_norm(projected, factor, offset).reshape(height, breadth, weight.shape[1])


def lift_levels(feature32, weights):
    (
        first_deconv,
        first_bias,
        mid_gain,
        mid_shift,
        second_deconv,
        second_bias,
        half_deconv,
        half_bias,
        laterals,
        level_gain,
        level_shift,
    ) = weights
    tokens = feature32.astype(jnp.bfloat16)
    height, breadth, channels = tokens.shape
    upsampled = expand_pixels(tokens, first_deconv, first_bias)
    upsampled = jax.nn.gelu(layer_norm(upsampled, mid_gain, mid_shift), approximate=False).astype(
        jnp.bfloat16
    )
    finest = expand_pixels(upsampled, second_deconv, second_bias).astype(jnp.bfloat16)
    middle = expand_pixels(tokens, half_deconv, half_bias).astype(jnp.bfloat16)
    coarse = jnp.max(tokens.reshape(height // 2, 2, breadth // 2, 2, channels), axis=(1, 3))
    sources = (finest, middle, tokens, coarse)
    return tuple(
        (
            lateral(
                sources[number], laterals[number], level_gain[number, 0], level_shift[number, 0]
            )
            for number in range(4)
        )
    )


def conv_three(padded, kernel):
    return lax.conv_general_dilated(
        padded[None],
        kernel,
        (1, 1),
        "VALID",
        dimension_numbers=("NHWC", "HWIO", "NHWC"),
        preferred_element_type=jnp.float32,
    )[0]


def flipped(kernel):
    return kernel[::-1, ::-1].transpose(0, 1, 3, 2)


def body(
    features,
    attn_hidden,
    first_deconv,
    first_bias,
    mid_gain,
    mid_shift,
    second_deconv,
    second_bias,
    half_deconv,
    half_bias,
    lateral_four,
    lateral_eight,
    lateral_sixteen,
    lateral_coarse,
    output_conv,
    level_gain,
    level_shift,
    cotangent_four,
    cotangent_eight,
    cotangent_sixteen,
    cotangent_coarse,
):
    per_device = features.shape[1]
    channels = features.shape[2]
    tile_cols = cotangent_sixteen.shape[2]
    breadth = tile_cols * lax.axis_size("tc")
    own_rows = per_device // breadth
    own_tokens = features[0].reshape(own_rows, breadth, channels)
    laterals = (lateral_four, lateral_eight, lateral_sixteen, lateral_coarse)
    cotangents = (cotangent_four, cotangent_eight, cotangent_sixteen, cotangent_coarse)
    first_full, half_full = (
        lax.all_gather(first_deconv, "segment", axis=0, tiled=True),
        lax.all_gather(half_deconv, "segment", axis=0, tiled=True),
    )
    passed = shifted(own_tokens, "segment", 1)
    tiled = lax.all_to_all(passed, "tc", split_axis=1, concat_axis=0, tiled=True)
    weights = (
        first_full,
        first_bias,
        mid_gain,
        mid_shift,
        second_deconv,
        second_bias,
        half_full,
        half_bias,
        laterals,
        level_gain,
        level_shift,
    )
    lifted, pullback = jax.vjp(
        lambda values: lift_levels(values, weights), tiled.astype(jnp.float32)
    )
    results = []
    gradients = []
    for number in range(4):
        activated = lifted[number].astype(jnp.bfloat16)
        padded = with_halo(activated, (("tr", 0), ("tc", 1)), 1)
        convolved = conv_three(padded, output_conv[number])
        normed, norm_pull = jax.vjp(
            lambda values: layer_norm(values, level_gain[number, 1], level_shift[number, 1]),
            convolved,
        )
        results.append(normed.astype(jnp.bfloat16)[None])
        back_norm = norm_pull(cotangents[number][0].astype(jnp.float32))[0].astype(jnp.bfloat16)
        back_pad = with_halo(back_norm, (("tr", 0), ("tc", 1)), 1)
        gradients.append(conv_three(back_pad, flipped(output_conv[number])))
    feature_back = pullback(tuple(gradients))[0].astype(jnp.bfloat16)
    returned = lax.all_to_all(feature_back, "tc", split_axis=0, concat_axis=1, tiled=True)
    returned_home = shifted(returned, "segment", 1)
    token_grads = returned_home.reshape(per_device, channels)
    partial_grad = lax.dot_general(
        attn_hidden[0], token_grads, (((0,), (0,)), ((), ())), preferred_element_type=jnp.float32
    )
    weight_grad = lax.psum_scatter(
        partial_grad, ("segment", "tr", "tc"), scatter_dimension=0, tiled=True
    )
    return (results[0], results[1], results[2], results[3], token_grads[None], weight_grad)


def solution(mesh):
    placed = (
        P("segment", ("tr", "tc"), None),
        P("segment", ("tr", "tc"), None),
        P("segment", None, None, None),
        P(),
        P(),
        P(),
        P(),
        P(),
        P("segment", None, None, None),
        P(),
        P(),
        P(),
        P(),
        P(),
        P(),
        P(),
        P(),
        P("segment", "tr", "tc", None),
        P("segment", "tr", "tc", None),
        P("segment", "tr", "tc", None),
        P("segment", "tr", "tc", None),
    )
    return jax.shard_map(
        body,
        mesh=mesh,
        in_specs=placed,
        out_specs=(
            P("segment", "tr", "tc", None),
            P("segment", "tr", "tc", None),
            P("segment", "tr", "tc", None),
            P("segment", "tr", "tc", None),
            P("segment", ("tr", "tc"), None),
            P(("segment", "tr", "tc"), None),
        ),
        check_vma=False,
    )
```

profile of v0, /device:TPU:1, one launch (start us, length us, event | category | flops | bytes accessed | tf_op | source)
XLA Modules:
  0.0 598.4 jit_solution(10540387198421138054)
XLA Ops:
  10.3 6.9 %collective-permute-done = bf16[2,64,1280]{2,1,0:T(8,128)(2,1)S(1)} collective-permute-done((bf16[2,64,1280]{2,1,0:T(8,128)(2,1)S(1)}, bf16[2,64,1280]{2,1,0:T(8,128)(2,1)S(1)}, u32[]{:S(2)}, u32[]{:S(2)}) %collective-permute-start) | collective-permute-done | bytes 327712 | tf_op jit(solution)/shard_map/ppermute | solution.py:11
  18.3 7.3 %all-to-all-start = ((bf16[2,64,1280]{2,0,1:T(2,128)(2,1)}), bf16[2,64,1280]{2,0,1:T(2,128)(2,1)S(1)}, u32[]{:S(2)}, u32[]{:S(2)}) async-start(bf16[2,64,1280]{2,0,1:T(2,128)(2,1)} %copy.491), calls=%async_computation | async-start | bytes 655360 | tf_op jit(solution)/shard_map/all_to_all | solution.py:143
  26.8 5.9 all-to-all-done
  38.8 4.6 collective-permute-start.13
  51.6 4.0 collective-permute-start.15
  65.4 4.3 collective-permute-start.21
  76.9 4.1 collective-permute-start.23
  86.3 5.7 collective-permute-start.17
  97.1 4.4 collective-permute-start.19
  110.9 15.1 %reshape.603 = bf16[1280,2560]{1,0:T(8,128)(2,1)} reshape(bf16[1280,2,2,640]{3,2,1,0:T(2,128)(2,1)} %all-gather.5.cloned.1.call-done) | data formatting | bytes 13107200 | tf_op jit(solution)/shard_map/jvp()/reshape | solution.py:38
  126.1 9.5 %copy.507 = bf16[1280,2560]{0,1:T(8,128)(2,1)} copy(bf16[1280,2560]{1,0:T(8,128)(2,1)} %reshape.603) | data formatting | bytes 13107200 | tf_op jit(solution)/shard_map/jvp()/reshape | solution.py:38
  135.5 5.1 fusion.60
  145.2 7.5 %collective-permute-start.5 = (bf16[1,16,256]{2,1,0:T(8,128)(2,1)}, bf16[1,16,256]{2,1,0:T(8,128)(2,1)}, u32[]{:S(2)}, u32[]{:S(2)}) collective-permute-start(bf16[1,16,256]{2,1,0:T(8,128)(2,1)} %get-tuple-element.99), channel_id=1, source_target_pairs={{0,8},{8,16},{16,24},{24,32},{32,40},{40,48},{48,56},{1,9},{9,17},... | collective-permute-start | bytes 24584 | tf_op jit(solution)/shard_map/ppermute | solution.py:21
  154.1 33.1 %all-gather.3.cloned.1.call-done = bf16[1280,2,2,640]{3,2,1,0:T(2,128)(2,1)} async-done(((bf16[640,2,2,640]{3,2,1,0:T(2,128)(2,1)}), bf16[1280,2,2,640]{3,2,1,0:T(2,128)(2,1)}) %all-gather.3.cloned.1.call-update) | async-done | bytes 6553616 | tf_op jit(solution)/shard_map/all_gather | solution.py:139
  187.3 15.0 %reshape.601 = bf16[1280,2560]{1,0:T(8,128)(2,1)} reshape(bf16[1280,2,2,640]{3,2,1,0:T(2,128)(2,1)} %all-gather.3.cloned.1.call-done) | data formatting | bytes 13107200 | tf_op jit(solution)/shard_map/jvp()/reshape | solution.py:38
  202.2 9.5 %copy.494 = bf16[1280,2560]{0,1:T(8,128)(2,1)} copy(bf16[1280,2560]{1,0:T(8,128)(2,1)} %reshape.601) | data formatting | bytes 13107200 | tf_op jit(solution)/shard_map/jvp()/reshape | solution.py:38
  211.8 5.3 fusion.195
  218.4 4.9 multiply_convert_fusion
  232.5 4.6 convert_element_type.152
  249.3 4.0 collective-permute-start.7
  270.5 4.3 collective-permute-start.25
  302.1 4.9 collective-permute-start.29
  327.6 5.4 fusion.2
  333.8 3.9 collective-permute-start.31
  345.3 6.4 %broadcast_multiply_fusion = (f32[64,8,5,256]{3,1,2,0:T(8,128)S(1)}, f32[64,8,5,256]{3,1,2,0:T(8,128)}) fusion(f32[256]{0:T(256)S(1)} %bitcast.382, bf16[4,3,3,256,256]{4,3,2,1,0:T(8,128)(2,1)} %param.35, bf16[66,1,7,2,256]{4,2,3,0,1:T(8,128)(2,1)S(1)} %slice.281, bf16[66,1,8,5,256]{4,2,3,0,1:T(8,128)(2,1)S(1)} %copy.541, pred[8,5]{0,1:T(8,128)(4,1)S(1)} %copy-done.118), kind=kOutput, calls=%fused_computation.73 | convolution fusion | flops 3026886656 | bytes 8248360 | tf_op jit(solution)/shard_map/conv_general_dilated | solution.py:93
  365.5 4.5 reshape.611
  374.0 4.6 reshape.612
  385.2 4.1 multiply_reduce_fusion.8
  391.8 5.0 fusion.5
  396.9 11.7 %all_to_all.33 = bf16[16,8,1280]{2,1,0:T(8,128)(2,1)S(1)} all-to-all(bf16[16,8,1280]{2,1,0:T(8,128)(2,1)S(1)} %fusion.5), channel_id=1, replica_groups=mesh['segment'=2,'tr'=8,'tc'=8] {'tc'}, dimensions={0} | all-to-all | bytes 655360 | tf_op jit(solution)/shard_map/all_to_all | solution.py:175
  409.2 8.2 %collective-permute-done.33 = bf16[2,64,1280]{2,1,0:T(8,128)(2,1)S(1)} collective-permute-done((bf16[2,64,1280]{2,1,0:T(8,128)(2,1)S(1)}, bf16[2,64,1280]{2,1,0:T(8,128)(2,1)S(1)}, u32[]{:S(2)}, u32[]{:S(2)}) %collective-permute-start.33) | collective-permute-done | bytes 327712 | tf_op jit(solution)/shard_map/ppermute | solution.py:11
  428.4 160.1 %all-reduce.3.cloned.1.call-done = f32[1280,1280]{0,1:T(8,128)} async-done(((f32[1280,1280]{0,1:T(8,128)}), f32[1280,1280]{0,1:T(8,128)}) %all-reduce.3.cloned.1.call-update) | async-done | bytes 6553616
  (523 shorter events, 197.9 us)
Async XLA Ops:
  7.2 103.7 %all-gather.5.cloned.1.call-start = ((), (), s32[]{:S(2)}) async-start(), calls=%async_computation.3 | async-start | bytes 9830400 | tf_op jit(solution)/shard_map/all_gather | solution.py:140
  7.9 179.3 %all-gather.3.cloned.1.call-start = ((), (), s32[]{:S(2)}) async-start(), calls=%async_computation.2 | async-start | bytes 9830400 | tf_op jit(solution)/shard_map/all_gather | solution.py:139
  8.3 9.0 %collective-permute-start = (bf16[2,64,1280]{2,1,0:T(8,128)(2,1)S(1)}, bf16[2,64,1280]{2,1,0:T(8,128)(2,1)S(1)}, u32[]{:S(2)}, u32[]{:S(2)}) collective-permute-start(bf16[2,64,1280]{2,1,0:T(8,128)(2,1)S(1)} %bitcast.393), channel_id=1, source_target_pairs={{0,64},{64,0},{1,65},{65,1},{2,66},{66,2},{3,67},{67,3},{4,68},{68... | collective-permute-start | bytes 983048 | tf_op jit(solution)/shard_map/ppermute | solution.py:11
  18.3 14.4 %all-to-all-start = ((bf16[2,64,1280]{2,0,1:T(2,128)(2,1)}), bf16[2,64,1280]{2,0,1:T(2,128)(2,1)S(1)}, u32[]{:S(2)}, u32[]{:S(2)}) async-start(bf16[2,64,1280]{2,0,1:T(2,128)(2,1)} %copy.491), calls=%async_computation | async-start | bytes 655360 | tf_op jit(solution)/shard_map/all_to_all | solution.py:143
  25.6 562.9 %all-reduce.3.cloned.1.call-start = ((), (), s32[]{:S(2)}) async-start(), calls=%async_computation.4 | async-start | bytes 13107200
  37.6 12.7 %collective-permute-start.14 = (bf16[1,4,256]{2,1,0:T(4,128)(2,1)}, bf16[1,4,256]{2,1,0:T(4,128)(2,1)}, u32[]{:S(2)}, u32[]{:S(2)}) collective-permute-start(bf16[1,4,256]{2,1,0:T(4,128)(2,1)} %get-tuple-element.117), channel_id=1, source_target_pairs={{8,0},{16,8},{24,16},{32,24},{40,32},{48,40},{56,48},{9,1},{17,9},... | collective-permute-start | bytes 6152 | tf_op jit(solution)/shard_map/ppermute | solution.py:22
  38.8 10.7 %collective-permute-start.13 = (bf16[1,4,256]{2,1,0:T(4,128)(2,1)S(1)}, bf16[1,4,256]{2,1,0:T(4,128)(2,1)}, u32[]{:S(2)}, u32[]{:S(2)}) collective-permute-start(bf16[1,4,256]{2,1,0:T(4,128)(2,1)S(1)} %get-tuple-element.118), channel_id=1, source_target_pairs={{0,8},{8,16},{16,24},{24,32},{32,40},{40,48},{48,56},{1,9},{9,17},... | collective-permute-start | bytes 6152 | tf_op jit(solution)/shard_map/ppermute | solution.py:21
  44.9 16.0 %collective-permute-start.9 = (bf16[1,8,256]{2,1,0:T(8,128)(2,1)}, bf16[1,8,256]{2,1,0:T(8,128)(2,1)}, u32[]{:S(2)}, u32[]{:S(2)}) collective-permute-start(bf16[1,8,256]{2,1,0:T(8,128)(2,1)} %get-tuple-element.107), channel_id=1, source_target_pairs={{0,8},{8,16},{16,24},{24,32},{32,40},{40,48},{48,56},{1,9},{9,17},... | collective-permute-start | bytes 12296 | tf_op jit(solution)/shard_map/ppermute | solution.py:21
  48.1 13.5 %collective-permute-start.10 = (bf16[1,8,256]{2,1,0:T(8,128)(2,1)}, bf16[1,8,256]{2,1,0:T(8,128)(2,1)}, u32[]{:S(2)}, u32[]{:S(2)}) collective-permute-start(bf16[1,8,256]{2,1,0:T(8,128)(2,1)} %get-tuple-element.108), channel_id=1, source_target_pairs={{8,0},{16,8},{24,16},{32,24},{40,32},{48,40},{56,48},{9,1},{17,9},... | collective-permute-start | bytes 12296 | tf_op jit(solution)/shard_map/ppermute | solution.py:22
  51.6 10.7 %collective-permute-start.15 = (bf16[10,1,256]{2,1,0:T(2,128)(2,1)}, bf16[10,1,256]{2,1,0:T(2,128)(2,1)S(1)}, u32[]{:S(2)}, u32[]{:S(2)}) collective-permute-start(bf16[10,1,256]{2,1,0:T(2,128)(2,1)} %get-tuple-element.111), channel_id=1, source_target_pairs={{0,1},{1,2},{2,3},{3,4},{4,5},{5,6},{6,7},{8,9},{9,10},{10,11},{11... | collective-permute-start | bytes 15368 | tf_op jit(solution)/shard_map/ppermute | solution.py:21
  65.4 11.5 %collective-permute-start.21 = (bf16[1,4,256]{2,1,0:T(4,128)(2,1)S(1)}, bf16[1,4,256]{2,1,0:T(4,128)(2,1)S(1)}, u32[]{:S(2)}, u32[]{:S(2)}) collective-permute-start(bf16[1,4,256]{2,1,0:T(4,128)(2,1)S(1)} %get-tuple-element.115), channel_id=1, source_target_pairs={{0,8},{8,16},{16,24},{24,32},{32,40},{40,48},{48,56},{1,9},{9,17},... | collective-permute-start | bytes 6152 | tf_op jit(solution)/shard_map/ppermute | solution.py:21
  71.0 12.1 %collective-permute-start.11 = (bf16[18,1,256]{2,0,1:T(8,128)(2,1)S(1)}, bf16[18,1,256]{2,0,1:T(8,128)(2,1)S(1)}, u32[]{:S(2)}, u32[]{:S(2)}) collective-permute-start(bf16[18,1,256]{2,0,1:T(8,128)(2,1)S(1)} %get-tuple-element.101), channel_id=1, source_target_pairs={{0,1},{1,2},{2,3},{3,4},{4,5},{5,6},{6,7},{8,9},{9,10},{10,11},{11... | collective-permute-start | bytes 27656 | tf_op jit(solution)/shard_map/ppermute | solution.py:21
  74.9 8.2 %collective-permute-start.12 = (bf16[18,1,256]{2,0,1:T(8,128)(2,1)S(1)}, bf16[18,1,256]{2,0,1:T(8,128)(2,1)S(1)}, u32[]{:S(2)}, u32[]{:S(2)}) collective-permute-start(bf16[18,1,256]{2,0,1:T(8,128)(2,1)S(1)} %get-tuple-element.102), channel_id=1, source_target_pairs={{1,0},{2,1},{3,2},{4,3},{5,4},{6,5},{7,6},{9,8},{10,9},{11,10},{12... | collective-permute-start | bytes 27656 | tf_op jit(solution)/shard_map/ppermute | solution.py:22
  76.9 16.5 %collective-permute-start.23 = (bf16[10,1,256]{2,1,0:T(2,128)(2,1)S(1)}, bf16[10,1,256]{2,1,0:T(2,128)(2,1)S(1)}, u32[]{:S(2)}, u32[]{:S(2)}) collective-permute-start(bf16[10,1,256]{2,1,0:T(2,128)(2,1)S(1)} %get-tuple-element.109), channel_id=1, source_target_pairs={{0,1},{1,2},{2,3},{3,4},{4,5},{5,6},{6,7},{8,9},{9,10},{10,11},{11... | collective-permute-start | bytes 15368 | tf_op jit(solution)/shard_map/ppermute | solution.py:21
  81.0 12.4 %collective-permute-start.24 = (bf16[10,1,256]{2,1,0:T(2,128)(2,1)S(1)}, bf16[10,1,256]{2,1,0:T(2,128)(2,1)S(1)}, u32[]{:S(2)}, u32[]{:S(2)}) collective-permute-start(bf16[10,1,256]{2,1,0:T(2,128)(2,1)S(1)} %get-tuple-element.110), channel_id=1, source_target_pairs={{1,0},{2,1},{3,2},{4,3},{5,4},{6,5},{7,6},{9,8},{10,9},{11,10},{12... | collective-permute-start | bytes 15368 | tf_op jit(solution)/shard_map/ppermute | solution.py:22
  86.3 10.1 %collective-permute-start.17 = (bf16[1,8,256]{2,1,0:T(8,128)(2,1)S(1)}, bf16[1,8,256]{2,1,0:T(8,128)(2,1)S(1)}, u32[]{:S(2)}, u32[]{:S(2)}) collective-permute-start(bf16[1,8,256]{2,1,0:T(8,128)(2,1)S(1)} %get-tuple-element.105), channel_id=1, source_target_pairs={{0,8},{8,16},{16,24},{24,32},{32,40},{40,48},{48,56},{1,9},{9,17},... | collective-permute-start | bytes 12296 | tf_op jit(solution)/shard_map/ppermute | solution.py:21
  97.1 8.0 %collective-permute-start.19 = (bf16[18,1,256]{2,1,0:T(2,128)(2,1)S(1)}, bf16[18,1,256]{2,1,0:T(2,128)(2,1)S(1)}, u32[]{:S(2)}, u32[]{:S(2)}) collective-permute-start(bf16[18,1,256]{2,1,0:T(2,128)(2,1)S(1)} %get-tuple-element.103), channel_id=1, source_target_pairs={{0,1},{1,2},{2,3},{3,4},{4,5},{5,6},{6,7},{8,9},{9,10},{10,11},{11... | collective-permute-start | bytes 27656 | tf_op jit(solution)/shard_map/ppermute | solution.py:21
  145.2 102.0 %collective-permute-start.5 = (bf16[1,16,256]{2,1,0:T(8,128)(2,1)}, bf16[1,16,256]{2,1,0:T(8,128)(2,1)}, u32[]{:S(2)}, u32[]{:S(2)}) collective-permute-start(bf16[1,16,256]{2,1,0:T(8,128)(2,1)} %get-tuple-element.99), channel_id=1, source_target_pairs={{0,8},{8,16},{16,24},{24,32},{32,40},{40,48},{48,56},{1,9},{9,17},... | collective-permute-start | bytes 24584 | tf_op jit(solution)/shard_map/ppermute | solution.py:21
  152.7 95.3 %collective-permute-start.6 = (bf16[1,16,256]{2,1,0:T(8,128)(2,1)}, bf16[1,16,256]{2,1,0:T(8,128)(2,1)}, u32[]{:S(2)}, u32[]{:S(2)}) collective-permute-start(bf16[1,16,256]{2,1,0:T(8,128)(2,1)} %get-tuple-element.100), channel_id=1, source_target_pairs={{8,0},{16,8},{24,16},{32,24},{40,32},{48,40},{56,48},{9,1},{17,9},... | collective-permute-start | bytes 24584 | tf_op jit(solution)/shard_map/ppermute | solution.py:22
  242.2 21.0 %collective-permute-start.1 = (bf16[1,32,256]{2,1,0:T(8,128)(2,1)}, bf16[1,32,256]{2,1,0:T(8,128)(2,1)}, u32[]{:S(2)}, u32[]{:S(2)}) collective-permute-start(bf16[1,32,256]{2,1,0:T(8,128)(2,1)} %get-tuple-element.89), channel_id=1, source_target_pairs={{0,8},{8,16},{16,24},{24,32},{32,40},{40,48},{48,56},{1,9},{9,17},... | collective-permute-start | bytes 49160 | tf_op jit(solution)/shard_map/ppermute | solution.py:21
  245.9 18.1 %collective-permute-start.2 = (bf16[1,32,256]{2,1,0:T(8,128)(2,1)}, bf16[1,32,256]{2,1,0:T(8,128)(2,1)}, u32[]{:S(2)}, u32[]{:S(2)}) collective-permute-start(bf16[1,32,256]{2,1,0:T(8,128)(2,1)} %get-tuple-element.90), channel_id=1, source_target_pairs={{8,0},{16,8},{24,16},{32,24},{40,32},{48,40},{56,48},{9,1},{17,9},... | collective-permute-start | bytes 49160 | tf_op jit(solution)/shard_map/ppermute | solution.py:22
  249.3 15.4 %collective-permute-start.7 = (bf16[34,1,256]{2,0,1:T(8,128)(2,1)}, bf16[34,1,256]{2,0,1:T(8,128)(2,1)}, u32[]{:S(2)}, u32[]{:S(2)}) collective-permute-start(bf16[34,1,256]{2,0,1:T(8,128)(2,1)} %get-tuple-element.95), channel_id=1, source_target_pairs={{0,1},{1,2},{2,3},{3,4},{4,5},{5,6},{6,7},{8,9},{9,10},{10,11},{11... | collective-permute-start | bytes 52232 | tf_op jit(solution)/shard_map/ppermute | solution.py:21
  253.3 11.4 %collective-permute-start.8 = (bf16[34,1,256]{2,0,1:T(8,128)(2,1)}, bf16[34,1,256]{2,0,1:T(8,128)(2,1)}, u32[]{:S(2)}, u32[]{:S(2)}) collective-permute-start(bf16[34,1,256]{2,0,1:T(8,128)(2,1)} %get-tuple-element.96), channel_id=1, source_target_pairs={{1,0},{2,1},{3,2},{4,3},{5,4},{6,5},{7,6},{9,8},{10,9},{11,10},{12... | collective-permute-start | bytes 52232 | tf_op jit(solution)/shard_map/ppermute | solution.py:22
  270.5 11.5 %collective-permute-start.25 = (bf16[1,16,256]{2,0,1:T(2,128)(2,1)S(1)}, bf16[1,16,256]{2,0,1:T(2,128)(2,1)S(1)}, u32[]{:S(2)}, u32[]{:S(2)}) collective-permute-start(bf16[1,16,256]{2,0,1:T(2,128)(2,1)S(1)} %get-tuple-element.97), channel_id=1, source_target_pairs={{0,8},{8,16},{16,24},{24,32},{32,40},{40,48},{48,56},{1,9},{9,17},... | collective-permute-start | bytes 24584 | tf_op jit(solution)/shard_map/ppermute | solution.py:21
  274.7 7.2 %collective-permute-start.26 = (bf16[1,16,256]{2,0,1:T(2,128)(2,1)S(1)}, bf16[1,16,256]{2,0,1:T(2,128)(2,1)S(1)}, u32[]{:S(2)}, u32[]{:S(2)}) collective-permute-start(bf16[1,16,256]{2,0,1:T(2,128)(2,1)S(1)} %get-tuple-element.98), channel_id=1, source_target_pairs={{8,0},{16,8},{24,16},{32,24},{40,32},{48,40},{56,48},{9,1},{17,9},... | collective-permute-start | bytes 24584 | tf_op jit(solution)/shard_map/ppermute | solution.py:22
  276.1 11.6 %collective-permute-start.3 = (bf16[66,1,256]{2,0,1:T(8,128)(2,1)S(1)}, bf16[66,1,256]{2,0,1:T(8,128)(2,1)S(1)}, u32[]{:S(2)}, u32[]{:S(2)}) collective-permute-start(bf16[66,1,256]{2,0,1:T(8,128)(2,1)S(1)} %get-tuple-element.85), channel_id=1, source_target_pairs={{0,1},{1,2},{2,3},{3,4},{4,5},{5,6},{6,7},{8,9},{9,10},{10,11},{11... | collective-permute-start | bytes 101384 | tf_op jit(solution)/shard_map/ppermute | solution.py:21
  280.0 7.7 %collective-permute-start.4 = (bf16[66,1,256]{2,0,1:T(8,128)(2,1)S(1)}, bf16[66,1,256]{2,0,1:T(8,128)(2,1)S(1)}, u32[]{:S(2)}, u32[]{:S(2)}) collective-permute-start(bf16[66,1,256]{2,0,1:T(8,128)(2,1)S(1)} %get-tuple-element.86), channel_id=1, source_target_pairs={{1,0},{2,1},{3,2},{4,3},{5,4},{6,5},{7,6},{9,8},{10,9},{11,10},{12... | collective-permute-start | bytes 101384 | tf_op jit(solution)/shard_map/ppermute | solution.py:22
  282.0 26.8 %collective-permute-start.27 = (bf16[34,1,256]{2,0,1:T(8,128)(2,1)S(1)}, bf16[34,1,256]{2,0,1:T(8,128)(2,1)S(1)}, u32[]{:S(2)}, u32[]{:S(2)}) collective-permute-start(bf16[34,1,256]{2,0,1:T(8,128)(2,1)S(1)} %get-tuple-element.93), channel_id=1, source_target_pairs={{0,1},{1,2},{2,3},{3,4},{4,5},{5,6},{6,7},{8,9},{9,10},{10,11},{11... | collective-permute-start | bytes 52232 | tf_op jit(solution)/shard_map/ppermute | solution.py:21
  285.7 23.1 %collective-permute-start.28 = (bf16[34,1,256]{2,0,1:T(8,128)(2,1)S(1)}, bf16[34,1,256]{2,0,1:T(8,128)(2,1)S(1)}, u32[]{:S(2)}, u32[]{:S(2)}) collective-permute-start(bf16[34,1,256]{2,0,1:T(8,128)(2,1)S(1)} %get-tuple-element.94), channel_id=1, source_target_pairs={{1,0},{2,1},{3,2},{4,3},{5,4},{6,5},{7,6},{9,8},{10,9},{11,10},{12... | collective-permute-start | bytes 52232 | tf_op jit(solution)/shard_map/ppermute | solution.py:22
  302.1 30.9 %collective-permute-start.29 = (bf16[1,32,256]{2,0,1:T(2,128)(2,1)}, bf16[1,32,256]{2,0,1:T(2,128)(2,1)}, u32[]{:S(2)}, u32[]{:S(2)}) collective-permute-start(bf16[1,32,256]{2,0,1:T(2,128)(2,1)} %get-tuple-element.87), channel_id=1, source_target_pairs={{0,8},{8,16},{16,24},{24,32},{32,40},{40,48},{48,56},{1,9},{9,17},... | collective-permute-start | bytes 49160 | tf_op jit(solution)/shard_map/ppermute | solution.py:21
  306.9 26.0 %collective-permute-start.30 = (bf16[1,32,256]{2,0,1:T(2,128)(2,1)}, bf16[1,32,256]{2,0,1:T(2,128)(2,1)}, u32[]{:S(2)}, u32[]{:S(2)}) collective-permute-start(bf16[1,32,256]{2,0,1:T(2,128)(2,1)} %get-tuple-element.88), channel_id=1, source_target_pairs={{8,0},{16,8},{24,16},{32,24},{40,32},{48,40},{56,48},{9,1},{17,9},... | collective-permute-start | bytes 49160 | tf_op jit(solution)/shard_map/ppermute | solution.py:22
  408.6 8.8 %collective-permute-start.33 = (bf16[2,64,1280]{2,1,0:T(8,128)(2,1)S(1)}, bf16[2,64,1280]{2,1,0:T(8,128)(2,1)S(1)}, u32[]{:S(2)}, u32[]{:S(2)}) collective-permute-start(bf16[2,64,1280]{2,1,0:T(8,128)(2,1)S(1)} %bitcast.350), channel_id=1, source_target_pairs={{0,64},{64,0},{1,65},{65,1},{2,66},{66,2},{3,67},{67,3},{4,68},{68... | collective-permute-start | bytes 983048 | tf_op jit(solution)/shard_map/ppermute | solution.py:11
  (128 other events, 1202.7 us)
Sparse Core Ops, SparseCore 0:
  9.7 89.0 all-gather.4
  100.4 86.8 all-gather.2
  421.5 166.9 all-reduce.2
where the time goes:
time: 608 us; the launch traced here: 598 us
  waiting for transfers between devices  220 us (36%)
  local copies, waits for them, and re-layouts  141 us (23%)
  starting transfers between devices  107 us (18%)
  matrix products  64.4 us (11%)
  other arithmetic  37.7 us (6%)
  between operations  16.7 us (3%)
  blocking collectives  11.7 us (2%)
    unnamed x4, waiting for transfers between devices  161 us
    ppermute x16, starting transfers between devices, with_halo(): before = lax.ppermute(last, axis, up)  70 us
    reshape x4, local copies, waits for them, and re-layouts, expand_pixels(): weight.reshape(channels, 4 * outward)  49.1 us
    all_gather x1, waiting for transfers between devices, body(): lax.all_gather(first_deconv, 'segment', axis=0, tiled=True)  33.1 us
    ppermute x16, starting transfers between devices, with_halo(): after = lax.ppermute(leading, axis, down)  27.3 us
    dot_general x6, matrix products, expand_pixels(): jnp.dot(pixels.reshape(height * breadth, channels), weight.reshape(channe...  27 us
    conv_general_dilated x8, matrix products, conv_three(): lax.conv_general_dilated(padded[None], kernel, (1, 1), 'VALID', dimension...  23.2 us
    ppermute x2, waiting for transfers between devices, shifted(): lax.ppermute(array, axis, [(i, (i + by) % devices) for i in range(devices)])  15.1 us
  transfers between devices with their start and end apart: 38, of which 8 were waited for; matrix products, arithmetic and copies ran while one was open for 28% of the time, Pallas kernels for 0%

commit v1 on v0

v1 whole, which is shorter than its diff:
```python
import jax
import jax.numpy as jnp
import numpy as np
from jax import lax
from jax.experimental import pallas as pl
from jax.experimental.pallas import tpu as pltpu
from jax.sharding import PartitionSpec as P

EPS = 1e-06
F32 = jnp.float32
BF16 = jnp.bfloat16
MESH = pl.DeviceIdType.MESH

ROWS, COLS = 16, 8
OWN, RING = 128, 64
TOK = OWN + RING
DIRS = ((-1, 0), (1, 0), (0, -1), (0, 1), (-1, -1), (-1, 1), (1, -1), (1, 1))
OPPOSITE = (1, 0, 3, 2, 7, 6, 5, 4)


def token_index(r, c):
    if not (-1 <= r <= ROWS and -1 <= c <= COLS):
        return None
    if 0 <= r < ROWS and 0 <= c < COLS:
        return r * COLS + c
    if 0 <= c < COLS:
        return OWN + (0 if r < 0 else 8) + c
    if 0 <= r < ROWS:
        return OWN + (16 if c < 0 else 32) + r
    return OWN + 48 + (0 if r < 0 else 2) + (0 if c < 0 else 1)


TOKENS_AT = [(r, c) for r in range(-1, ROWS + 1) for c in range(-1, COLS + 1)]


def shift_matrices():
    out = np.zeros((3, 3, TOK, TOK), np.float32)
    for r, c in TOKENS_AT:
        for dy in range(-1, 2):
            for dx in range(-1, 2):
                there = token_index(r + dy, c + dx)
                if there is not None:
                    out[dy + 1, dx + 1, token_index(r, c), there] = 1
    return out


def ring_pick():
    out = np.zeros((RING, 128), np.float32)
    for c in range(8):
        out[c, 0 * 16 + 8 + c] = 1
        out[8 + c, 1 * 16 + c] = 1
    for r in range(16):
        out[16 + r, 2 * 16 + r] = 1
        out[32 + r, 3 * 16 + r] = 1
    out[48, 4 * 16 + 15] = 1
    out[49, 5 * 16 + 8] = 1
    out[50, 6 * 16 + 7] = 1
    out[51, 7 * 16 + 0] = 1
    return out


def column_pick():
    out = np.zeros((32, 128), np.float32)
    for r in range(16):
        out[r, r * 8] = 1
        out[16 + r, r * 8 + 7] = 1
    return out


SMALL_SIZE = (16, 16, 32, 32, 16, 16, 16, 16)
SMALL_AT = tuple(int(v) for v in np.cumsum((0,) + SMALL_SIZE)[:8])
SMALL = sum(SMALL_SIZE)


def edge_pixels(height, width, k):
    dy, dx = DIRS[k]
    rows = range(height) if dy == 0 else ([0] if dy < 0 else [height - 1])
    cols = range(width) if dx == 0 else ([0] if dx < 0 else [width - 1])
    return [(r, c) for r in rows for c in cols]


def small_send():
    out = np.zeros((SMALL, 160), np.float32)
    for k in range(8):
        at = SMALL_AT[k]
        for r, c in edge_pixels(16, 8, k):
            out[at, r * 8 + c] = 1
            at += 1
        for r, c in edge_pixels(8, 4, k):
            out[at, 128 + r * 4 + c] = 1
            at += 1
    return out


def halo_slot(height, width, r, c):
    k = DIRS.index(((r >= height) - (r < 0), (c >= width) - (c < 0)))
    return k, edge_pixels(height, width, OPPOSITE[k]).index((r % height, c % width))


def small_taps():
    out = np.zeros((9, 160, 160 + SMALL), np.float32)
    for base, height, width in ((0, 16, 8), (128, 8, 4)):
        for t in range(9):
            for r in range(height):
                for c in range(width):
                    rr, cc = r + t // 3 - 1, c + t % 3 - 1
                    if 0 <= rr < height and 0 <= cc < width:
                        out[t, base + r * width + c, base + rr * width + cc] = 1
                    else:
                        k, place = halo_slot(height, width, rr, cc)
                        place += len(edge_pixels(16, 8, OPPOSITE[k])) if base else 0
                        out[t, base + r * width + c, 160 + SMALL_AT[k] + place] = 1
    return out


COT_SIZE = (48, 48, 96, 96, 16, 16, 16, 16)
COT_AT = tuple(int(v) for v in np.cumsum((0,) + COT_SIZE)[:8])
COT = sum(COT_SIZE)


def cot_send():
    index = np.full((COT,), -1)
    for k in range(8):
        at = COT_AT[k]
        for r, c in edge_pixels(64, 32, k):
            index[at] = r * 32 + c
            at += 1
        for r, c in edge_pixels(32, 16, k):
            index[at] = 2048 + r * 16 + c
            at += 1
    return index


def cot_ring(n):
    height, width = ROWS * n, COLS * n
    out = np.zeros((n, n, RING, COT), np.float32)
    for r, c in TOKENS_AT:
        if 0 <= r < ROWS and 0 <= c < COLS:
            continue
        for ph in range(n):
            for pw in range(n):
                y, x = r * n + ph, c * n + pw
                if -1 <= y <= height and -1 <= x <= width:
                    k, place = halo_slot(height, width, y, x)
                    place += len(edge_pixels(64, 32, OPPOSITE[k])) if n == 2 else 0
                    out[ph, pw, token_index(r, c) - OWN, COT_AT[k] + place] = 1
    return out.reshape(n * n * RING, COT)


def interleave(n):
    tokens = 256 // n
    out = np.zeros((256, 256), np.float32)
    for t in range(tokens):
        for p in range(n):
            out[t * n + p, p * tokens + t] = 1
    return out


def quad_pick():
    out = np.zeros((4, 32, 128), np.float32)
    for q in range(4):
        for r in range(8):
            for c in range(4):
                out[q, r * 4 + c, (2 * r + q // 2) * 8 + 2 * c + q % 2] = 1
    return out


def chunk_split():
    out = np.zeros((320, 320), np.float32)
    for e in range(80):
        for p in range(4):
            out[p * 80 + e, e * 4 + p] = 1
    return out


def cot_pick():
    index = cot_send()
    out = np.zeros((COT, 2560), np.float32)
    for row, at in enumerate(index):
        if at >= 0:
            out[row, at] = 1
    return out


def const(array):
    return jnp.asarray(array, BF16)


def mm(a, b):
    return jnp.dot(a, b, preferred_element_type=F32)


def mt(a, b):
    return lax.dot_general(a, b, (((1,), (1,)), ((), ())), preferred_element_type=F32)


def pick(selection, a):
    return mm(selection, a).astype(BF16)


def normed(values):
    centre = jnp.mean(values, axis=-1, keepdims=True)
    values = values - centre
    scale = lax.rsqrt(jnp.mean(values * values, axis=-1, keepdims=True) + EPS)
    return values * scale, scale


def norm_back(unit, scale, grad):
    return scale * (
        grad
        - jnp.mean(grad, axis=-1, keepdims=True)
        - unit * jnp.mean(grad * unit, axis=-1, keepdims=True)
    )


def place():
    return lax.axis_index("segment"), lax.axis_index("tr"), lax.axis_index("tc")


def neighbour(k, s, tr, tc):
    dy, dx = DIRS[k]
    return (s, (tr + dy + 8) % 8, (tc + dx + 8) % 8)


def exists_mask(rows, spans):
    _, tr, tc = place()
    row = lax.broadcasted_iota(jnp.int32, (rows, 1), 0)
    mask = jnp.ones((rows, 1), F32)
    for k, lo, hi in spans:
        if k is None:
            there = 0.0
        else:
            dy, dx = DIRS[k]
            inside = (tr + dy >= 0) & (tr + dy < 8) & (tc + dx >= 0) & (tc + dx < 8)
            there = jnp.where(inside, 1.0, 0.0)
        mask = jnp.where((row >= lo) & (row < hi), there, mask)
    return mask


RING_SPANS = (
    (0, 128, 136), (1, 136, 144), (2, 144, 160), (3, 160, 176),
    (4, 176, 177), (5, 177, 178), (6, 178, 179), (7, 179, 180), (None, 180, 192),
)
SMALL_SPANS = tuple((k, SMALL_AT[k], SMALL_AT[k] + SMALL_SIZE[k]) for k in range(8))


def signal_all(peers):
    barrier = pltpu.get_barrier_semaphore()
    for peer in peers:
        pl.semaphore_signal(barrier, inc=1, device_id=peer, device_id_type=MESH)


def wait_all(peers):
    pl.semaphore_wait(pltpu.get_barrier_semaphore(), len(peers))


class Copies:
    def __init__(self, send, recv):
        self.send, self.recv, self.used, self.unsent = send, recv, 0, []

    def start(self, src, dst, peer):
        k, self.used = self.used, self.used + 1
        copy = pltpu.make_async_remote_copy(
            src_ref=src,
            dst_ref=dst,
            send_sem=self.send.at[k],
            recv_sem=self.recv.at[k],
            device_id=peer,
            device_id_type=MESH,
        )
        copy.start()
        self.unsent.append(copy)
        return copy

    def finish(self):
        for copy in self.unsent:
            copy.wait_send()


SPLIT = 1792


def split_product(row, weight):
    total = 0.0
    for _ in range(3):
        piece = row.astype(BF16)
        total = total + mm(piece, weight)
        row = row - piece.astype(F32)
    return total


def front_kernel(
    feat, attn, first, half, k2t, l4, l8, l16, lc, b2, bh, conv, gains, offsets, cot4, cot8, cot16, cotc,
    split, columns, ring_sel, edges, taps, quad, quad_t, cot_sel, cot_ring4, cot_ring8,
    wo, wr, xe, c2t, bias4, bias8, ring4, ring8, attn_t, dx_small, lev16, levc,
    w_own, w_rem, xa, aa, xt, at, xh, sides, small, small_h, back, back_h, cotm, cot_h, attn_c, attn_h, send, recv,
):
    s, tr, tc = place()
    other = 1 - s
    x_hi, y, z, core = tr // 4, tr % 4, tc // 2, tc % 2
    turn = 1 - 2 * core
    far = (other, (1 - x_hi) * 4 + y, tc)
    sibling = (s, tr, tc + turn)
    z_ahead = (s, tr, (z + turn + 4) % 4 * 2 + core)
    z_behind = (s, tr, (z - turn + 4) % 4 * 2 + core)
    y_ahead = (s, x_hi * 4 + (y + turn + 4) % 4, tc)
    y_behind = (s, x_hi * 4 + (y - turn + 4) % 4, tc)
    around = [neighbour(k, s, tr, tc) for k in range(8)]
    across = [(other, tr, (tc + o) % 8) for o in range(8)]
    along = [(s, tr, (tc + o) % 8) for o in range(1, 8)]
    peers = across + [far, sibling, z_ahead, z_behind, y_ahead, y_behind] + around + along
    signal_all(peers)
    copies = Copies(send, recv)

    def relayout(chunk):
        rows = pl.ds(pl.multiple_of(chunk * 80, 80), 80)
        block = mm(split[...], first[rows].reshape(320, 640)).astype(BF16)
        product = mm(half[rows].reshape(320, 640), l8[...]).astype(BF16)
        product = mm(split[...], product).astype(BF16)
        for p in range(4):
            w_own[chunk, :, 640 * p : 640 * p + 640] = block[80 * p : 80 * p + 80]
            w_own[chunk, :, 2560 + 256 * p : 2816 + 256 * p] = product[80 * p : 80 * p + 80]

    for j in range(8):
        for i in range(2):
            xa[j, 8 * i : 8 * i + 8] = feat[64 * i + 8 * j : 64 * i + 8 * j + 8]
            aa[j, 8 * i : 8 * i + 8] = attn[64 * i + 8 * j : 64 * i + 8 * j + 8]
    relayout(z)
    wait_all(peers)
    mine = pl.ds(pl.multiple_of(core * SPLIT, 128), SPLIT)
    x_copies = [copies.start(xa.at[(tc + o) % 8], xt.at[tc], across[o]) for o in range(8)]
    z_first = copies.start(w_own.at[z, :, mine], w_rem.at[z, :, mine], far)
    relayout(4 + y)
    y_first = copies.start(w_own.at[4 + y, :, mine], w_rem.at[4 + y, :, mine], far)
    pixels = jnp.concatenate([cot4[...].reshape(2048, 256), cot8[...].reshape(512, 256)])
    cotm[...] = pick(cot_sel[...], pixels)
    cot_copies = [
        copies.start(
            cotm.at[pl.ds(COT_AT[k], COT_SIZE[k])],
            cot_h.at[pl.ds(COT_AT[OPPOSITE[k]], COT_SIZE[k])],
            around[k],
        )
        for k in range(8)
    ]

    @pl.loop(1, 4)
    def rest(i):
        relayout((z + i) % 4)
        relayout(4 + (y + i) % 4)

    shared = []

    def share(chunk):
        shared.append(copies.start(w_rem.at[chunk, :, mine], w_rem.at[chunk, :, mine], sibling))

    for copy in x_copies:
        copy.wait_recv()
    x = xt[...].reshape(OWN, 1280)
    sides[...] = pick(columns[...], x).reshape(2, 16, 1280)
    sources = (xt.at[0], xt.at[7], sides.at[0], sides.at[1], xt.at[0], xt.at[0], xt.at[7], xt.at[7])
    halo_copies = [copies.start(sources[k], xh.at[OPPOSITE[k]], around[k]) for k in range(8)]
    quads = [pick(quad[q], x) for q in range(4)]
    coarse = jnp.maximum(jnp.maximum(quads[0], quads[1]), jnp.maximum(quads[2], quads[3]))
    units = [normed(mm(x, l16[...])), normed(mm(coarse, lc[...]))]
    laterals = jnp.concatenate(
        [(units[i][0] * gains[2 + i, 0:1] + offsets[2 + i, 0:1]).astype(BF16) for i in range(2)]
    )

    def exchange(rows, message, halo):
        message[...] = pick(edges[...], rows)
        return [
            copies.start(
                message.at[pl.ds(SMALL_AT[k], SMALL_SIZE[k])],
                halo.at[pl.ds(SMALL_AT[OPPOSITE[k]], SMALL_SIZE[k])],
                around[k],
            )
            for k in range(8)
        ]

    def small_conv(rows, halo, product, order):
        both = jnp.concatenate([rows, (halo[...] * exists_mask(SMALL, SMALL_SPANS)).astype(BF16)])
        sums = [jnp.zeros((128, 256), F32), jnp.zeros((32, 256), F32)]
        for t in range(9):
            moved = pick(taps[t], both)
            for i, (lo, hi) in enumerate(((0, 128), (128, 160))):
                sums[i] = sums[i] + product(moved[lo:hi], conv[2 + i, order(t)])
        return sums

    small_copies = exchange(laterals, small, small_h)
    z_first.wait_recv()
    z_up = copies.start(w_rem.at[z, :, mine], w_rem.at[z, :, mine], z_ahead)
    z_down = copies.start(w_rem.at[z, :, mine], w_rem.at[z, :, mine], z_behind)
    share(z)
    a_copies = [copies.start(aa.at[(tc + o) % 8], at.at[tc], across[o]) for o in range(8)]
    for p in range(4):
        c2t[p] = lax.dot_general(
            l4[...], k2t[p], (((0,), (0,)), ((), ())), preferred_element_type=F32
        ).astype(BF16)
    bias4[...] = split_product(b2[...], l4[...])
    bias8[...] = split_product(bh[...], l8[...])
    y_first.wait_recv()
    y_up = copies.start(w_rem.at[4 + y, :, mine], w_rem.at[4 + y, :, mine], y_ahead)
    y_down = copies.start(w_rem.at[4 + y, :, mine], w_rem.at[4 + y, :, mine], y_behind)
    share(4 + y)
    for copy in small_copies:
        copy.wait_recv()
    sums = small_conv(laterals, small_h, mm, lambda t: t)
    grads = []
    for i, (cot, level_out) in enumerate(((cot16, lev16), (cotc, levc))):
        unit, scale = normed(sums[i])
        gain = gains[2 + i, 1:2]
        level_out[...] = (unit * gain + offsets[2 + i, 1:2]).astype(BF16)
        grads.append(norm_back(unit, scale, cot[...].astype(F32) * gain).astype(BF16))
    grads = jnp.concatenate(grads)
    back_copies = exchange(grads, back, back_h)

    z_ring = [(z - turn + 4) % 4, (z + turn + 4) % 4, (z + 2) % 4]
    y_ring = [4 + (y - turn + 4) % 4, 4 + (y + turn + 4) % 4, 4 + (y + 2) % 4]
    z_up.wait_recv()
    z_on = copies.start(w_rem.at[z_ring[0], :, mine], w_rem.at[z_ring[0], :, mine], z_ahead)
    share(z_ring[0])
    z_down.wait_recv()
    share(z_ring[1])
    y_up.wait_recv()
    y_on = copies.start(w_rem.at[y_ring[0], :, mine], w_rem.at[y_ring[0], :, mine], y_ahead)
    share(y_ring[0])
    y_down.wait_recv()
    share(y_ring[1])

    for copy in a_copies:
        copy.wait_recv()
    tile = at[...].reshape(OWN, 1280)
    row = lax.broadcasted_iota(jnp.int32, (1280, 256), 0)
    column = lax.broadcasted_iota(jnp.int32, (1280, 256), 1)
    row = jnp.where(column % 16 < 10, row - column // 16 * 80 - column % 16, -1)

    @pl.loop(0, 8)
    def attn_columns(j):
        attn_c[j] = mm(tile, (row == 10 * j).astype(F32).astype(BF16)).astype(BF16)

    attn_copies = [
        copies.start(attn_c.at[(tc + o) % 8], attn_h.at[tc], along[o - 1]) for o in range(1, 8)
    ]
    attn_h[tc] = attn_c[tc]

    for copy in back_copies:
        copy.wait_recv()
    sums = small_conv(grads, back_h, mt, lambda t: 8 - t)
    steps = []
    for i, weight in enumerate((l16, lc)):
        unit, scale = units[i]
        steps.append(mt(norm_back(unit, scale, sums[i] * gains[2 + i, 0:1]).astype(BF16), weight[...]))
    hits = [jnp.where(q.astype(F32) == coarse.astype(F32), 1.0, 0.0) for q in quads]
    portion = steps[1] / (hits[0] + hits[1] + hits[2] + hits[3])
    total = steps[0]
    for q in range(4):
        total = total + mm(quad_t[q], (hits[q] * portion).astype(BF16))
    dx_small[...] = total

    for copy in halo_copies + cot_copies:
        copy.wait_recv()
    xe[:OWN] = x
    xe[OWN:] = pick(ring_sel[...], xh[...].reshape(128, 1280))
    ring4[...] = pick(cot_ring4[...], cot_h[...]).reshape(4, 4, RING, 256)
    ring8[...] = pick(cot_ring8[...], cot_h[...]).reshape(2, 2, RING, 256)
    wo[...] = w_own[...]
    z_on.wait_recv()
    share(z_ring[2])
    y_on.wait_recv()
    share(y_ring[2])
    for copy in attn_copies:
        copy.wait_recv()
    for j in range(8):
        attn_t[:, 128 * j : 128 * j + 128] = attn_h[j].T
    for copy in shared:
        copy.wait_recv()
    wr[...] = w_rem[...]
    copies.finish()


def shape(dims, dtype=BF16):
    return jax.ShapeDtypeStruct(dims, dtype)


def call(kernel, outs, scratch, args, collective_id=None):
    vmem = pl.BlockSpec(memory_space=pltpu.VMEM)
    params = {"vmem_limit_bytes": 60 * 2**20}
    if collective_id is not None:
        params.update(collective_id=collective_id, has_side_effects=True)
    return pl.pallas_call(
        kernel,
        out_shape=outs,
        in_specs=[vmem] * len(args),
        out_specs=[vmem] * len(outs),
        scratch_shapes=scratch,
        compiler_params=pltpu.CompilerParams(**params),
    )(*args)


def buffer(*dims):
    return pltpu.VMEM(dims, BF16)


def front(*args):
    copies = 8 + 2 + 8 + 8 + 8 + 4 + 8 + 8 + 8 + 2 + 7
    return call(
        front_kernel,
        [
            shape((8, 80, 3584)), shape((8, 80, 3584)), shape((TOK, 1280)), shape((4, 256, 640)),
            shape((1, 256), F32), shape((1, 256), F32), shape((4, 4, RING, 256)), shape((2, 2, RING, 256)),
            shape((256, 1024)), shape((OWN, 1280), F32), shape((128, 256)), shape((32, 256)),
        ],
        [
            buffer(8, 80, 3584), buffer(8, 80, 3584),
            buffer(8, 16, 1280), buffer(8, 16, 1280), buffer(8, 16, 1280), buffer(8, 16, 1280),
            buffer(8, 16, 1280), buffer(2, 16, 1280),
            buffer(SMALL, 256), buffer(SMALL, 256), buffer(SMALL, 256), buffer(SMALL, 256),
            buffer(COT, 256), buffer(COT, 256), buffer(8, OWN, 256), buffer(8, OWN, 256),
            pltpu.SemaphoreType.DMA((copies,)), pltpu.SemaphoreType.DMA((copies,)),
        ],
        args,
        collective_id=0,
    )


def erf(x):
    x = jnp.clip(x, -3.832506856900711, 3.832506856900711)
    square = x * x
    over = jnp.full_like(x, 0.00022905065861350646)
    for c in (0.0034082910107109506, 0.050955695062380861, 0.18520832239976145, 1.128379143519084):
        over = over * square + c
    under = jnp.full_like(x, -1.1791602954361697e-7)
    for c in (0.000023547966471313185, 0.0010179625278914885, 0.014070470171167667,
              0.11098505178285362, 0.49746925110067538, 1.0):
        under = under * square + c
    return x * over / under


def fill_shifted(padded, n, shifts):
    for i in range(n + 2):
        for j in range(n + 2):
            dy, dx = (i - 1) // n, (j - 1) // n
            if dy or dx:
                source = padded[(i - 1) % n + 1, (j - 1) % n + 1]
                padded[i, j] = mm(shifts[3 * dy + dx + 4], source).astype(BF16)


def pyramid_level(n, lat, back, unit, scale, conv, cot, ring, out, gains, offsets, keep, shifts, split, done):
    groups = n * n // 8 if n == 4 else 1
    rows = ROWS // groups
    fill_shifted(lat, n, shifts)

    @pl.loop(0, n)
    def forward(ph):
        acc = jnp.zeros((n * TOK, 256), F32)
        for t in range(9):
            dy, dx = t // 3, t % 3
            block = lat[ph + dy, dx : dx + n].reshape(n * TOK, 256)
            acc = acc + mm(block, conv[t])
        pieces = []
        for g in range(groups):
            block = cot[pl.ds(rows * g, rows), ph].reshape(256, 256)
            pieces.append(mm(split[1], block))
        tokens = 256 // n
        results = []
        for pw in range(n):
            values, size = normed(acc[pw * TOK : pw * TOK + TOK])
            results.append((values[:OWN] * gains[1:2] + offsets[1:2]).astype(BF16))
            own = [piece[pw * tokens : pw * tokens + tokens] for piece in pieces]
            grads = jnp.concatenate(own + [ring[ph, pw].astype(F32)], axis=0)
            grads = norm_back(values, size, grads * gains[1:2])
            back[ph + 1, pw + 1] = (grads * keep).astype(BF16)
        for g in range(groups):
            block = jnp.concatenate([r[g * tokens : g * tokens + tokens] for r in results], axis=0)
            block = mm(split[0], block).astype(BF16)
            out[pl.ds(rows * g, rows), ph] = block.reshape(rows, 8 * n, 256)

    fill_shifted(back, n, shifts)

    @pl.loop(0, n)
    def backward(ph):
        acc = jnp.zeros((n * OWN, 256), F32)
        for t in range(9):
            dy, dx = t // 3, t % 3
            block = jnp.concatenate([back[ph + dy, dx + pw, :OWN] for pw in range(n)], axis=0)
            acc = acc + mt(block, conv[8 - t])
        for pw in range(n):
            grads = acc[pw * OWN : pw * OWN + OWN] * gains[0:1]
            done(ph, pw, norm_back(unit[ph, pw], scale[ph, pw], grads).astype(BF16))


def levels_kernel(
    xe, wo, wr, second, conv, cot4, cot8, ring4, ring8, dx_small, shifts, split4, split8,
    bias1, gain_m, shift_m, bias4, bias8, gains, offsets,
    out4, out8, dx,
    up, unit_u, slope_u, scale_u, lat4, back4, unit4, scale4, lat8, back8, unit8, scale8, d4, dfull,
):
    keep = exists_mask(TOK, RING_SPANS)
    s, _, _ = place()
    own = pl.ds(pl.multiple_of(640 * s, 128), 640)
    other = pl.ds(pl.multiple_of(640 - 640 * s, 128), 640)
    xo, xr = xe[:, own], xe[:, other]
    for p in range(4):
        cols = pl.ds(640 * p, 640)
        pre = mm(xo, wo[:, cols]) + mm(xr, wr[:, cols]) + bias1[...]
        unit, size = normed(pre)
        before = unit * gain_m[...] + shift_m[...]
        cdf = 0.5 * (1 + erf(before * (0.5**0.5)))
        up[p] = (before * cdf).astype(BF16)
        inner = before[:OWN]
        unit_u[p] = unit[:OWN]
        scale_u[p] = size[:OWN]
        slope_u[p] = (cdf[:OWN] + inner * jnp.exp(-0.5 * inner * inner) * (1 / np.sqrt(2 * np.pi))) * gain_m[...]
    for p in range(4):
        for q in range(4):
            ph, pw = 2 * (p // 2) + q // 2, 2 * (p % 2) + q % 2
            pre = mt(up[p], second[q]) + bias4[...]
            unit, size = normed(pre)
            unit4[ph, pw] = unit[:OWN]
            scale4[ph, pw] = size[:OWN]
            lat4[ph + 1, pw + 1] = ((unit * gains[0, 0:1] + offsets[0, 0:1]) * keep).astype(BF16)
    for p in range(4):
        cols = pl.ds(2560 + 256 * p, 256)
        pre = mm(xo, wo[:, cols]) + mm(xr, wr[:, cols]) + bias8[...]
        unit, size = normed(pre)
        unit8[p // 2, p % 2] = unit[:OWN]
        scale8[p // 2, p % 2] = size[:OWN]
        lat8[p // 2 + 1, p % 2 + 1] = ((unit * gains[1, 0:1] + offsets[1, 0:1]) * keep).astype(BF16)

    def done4(ph, pw, grads):
        d4[2 * (ph // 2) + pw // 2, 2 * (ph % 2) + pw % 2] = grads

    def done8(ph, pw, grads):
        d8[2 * ph + pw] = grads

    d8 = d4.at[4]
    pyramid_level(
        4, lat4, back4, unit4, scale4, conv.at[0], cot4, ring4, out4, gains[0], offsets[0], keep, shifts, split4, done4
    )
    pyramid_level(
        2, lat8, back8, unit8, scale8, conv.at[1], cot8, ring8, out8, gains[1], offsets[1], keep, shifts, split8, done8
    )
    dup = jnp.zeros((4 * OWN, 640), F32)
    for q in range(4):
        block = jnp.concatenate([d4[p, q] for p in range(4)], axis=0)
        dup = dup + mm(block, second[q])
    for p in range(4):
        grads = norm_back(unit_u[p], scale_u[p], dup[p * OWN : p * OWN + OWN] * slope_u[p])
        dfull[:, 640 * p : 640 * p + 640] = grads.astype(BF16)
        dfull[:, 2560 + 256 * p : 2816 + 256 * p] = d4[4, p]
    dx[:, own] = (mt(dfull[...], wo[...]) + dx_small[:, own]).astype(BF16)
    dx[:, other] = (mt(dfull[...], wr[...]) + dx_small[:, other]).astype(BF16)


def levels(*args):
    def wide(*dims):
        return pltpu.VMEM(dims, F32)

    return call(
        levels_kernel,
        [shape((16, 4, 32, 256)), shape((16, 2, 16, 256)), shape((OWN, 1280))],
        [
            buffer(4, TOK, 640), wide(4, OWN, 640), wide(4, OWN, 640), wide(4, OWN, 1),
            buffer(6, 6, TOK, 256), buffer(6, 6, TOK, 256), wide(4, 4, OWN, 256), wide(4, 4, OWN, 1),
            buffer(4, 4, TOK, 256), buffer(4, 4, TOK, 256), wide(2, 2, OWN, 256), wide(2, 2, OWN, 1),
            buffer(5, 4, OWN, 256), buffer(OWN, 3584),
        ],
        args,
    )


def last_kernel(dx, attn_t, grads, weight, mine, home, tiles, part, parts, send, recv):
    s, tr, tc = place()
    other, me = 1 - s, s * 8 + tr
    sibling = (s, tr, tc + 1 - 2 * (tc % 2))
    ring = [(s, tr, (tc + 2 * j) % 8) for j in (1, 3, 2)]
    across = [(other, tr, (tc + o) % 8) for o in range(8)]
    plane = [((me + o) % 16 // 8, (me + o) % 8, tc) for o in range(1, 16)]
    peers = across + ring + [sibling] + plane
    signal_all(peers)
    copies = Copies(send, recv)
    mine[...] = dx[...].reshape(8, 16, 1280)
    wait_all(peers)
    received = [copies.start(mine, tiles.at[tc], peer) for peer in ring]
    shared = [copies.start(mine, tiles.at[tc], sibling)]
    homes = [copies.start(mine.at[(tc + o) % 8], home.at[tc], across[o]) for o in range(8)]
    tiles[tc] = mine[...]
    for copy, j in zip(received, (1, 3, 2)):
        copy.wait_recv()
        slot = (tc + 8 - 2 * j) % 8
        shared.append(copies.start(tiles.at[slot], tiles.at[slot], sibling))
    for copy in shared:
        copy.wait_recv()
    product = mm(attn_t[...], tiles[...].reshape(8 * OWN, 1280))
    part[...] = product.astype(BF16).reshape(16, 16, 1280)
    sums = [copies.start(part.at[(me + o) % 16], parts.at[me], plane[o - 1]) for o in range(1, 16)]
    parts[me] = part[me]
    for copy in homes:
        copy.wait_recv()
    for j in range(8):
        for i in range(2):
            grads[64 * i + 8 * j : 64 * i + 8 * j + 8] = home[j, 8 * i : 8 * i + 8]
    for copy in sums:
        copy.wait_recv()
    total = parts[0].astype(F32)
    for j in range(1, 16):
        total = total + parts[j].astype(F32)
    weight[...] = total[:10]
    copies.finish()


def last(*args):
    copies = 3 + 1 + 8 + 3 + 15
    return call(
        last_kernel,
        [shape((OWN, 1280)), shape((10, 1280), F32)],
        [
            buffer(8, 16, 1280), buffer(8, 16, 1280), buffer(8, 8, 16, 1280),
            buffer(16, 16, 1280), buffer(16, 16, 1280),
            pltpu.SemaphoreType.DMA((copies,)), pltpu.SemaphoreType.DMA((copies,)),
        ],
        args,
        collective_id=1,
    )


def body(
    features,
    attn_hidden,
    first_deconv,
    first_bias,
    mid_gain,
    mid_shift,
    second_deconv,
    second_bias,
    half_deconv,
    half_bias,
    lateral_four,
    lateral_eight,
    lateral_sixteen,
    lateral_coarse,
    output_conv,
    level_gain,
    level_shift,
    cotangent_four,
    cotangent_eight,
    cotangent_sixteen,
    cotangent_coarse,
):
    k2t = second_deconv.transpose(1, 2, 3, 0).reshape(4, 320, 640)
    conv = output_conv.reshape(4, 9, 256, 256)
    cot4 = cotangent_four.reshape(16, 4, 32, 256)
    cot8 = cotangent_eight.reshape(16, 2, 16, 256)
    quads = quad_pick()
    rings = cot_ring(4), cot_ring(2)
    wo, wr, xe, c2t, bias4, bias8, ring4, ring8, attn_t, dx_small, lev16, levc = front(
        features[0], attn_hidden[0], first_deconv, half_deconv, k2t,
        lateral_four, lateral_eight, lateral_sixteen, lateral_coarse,
        second_bias.reshape(1, 320), half_bias.reshape(1, 640),
        conv, level_gain, level_shift, cot4, cot8,
        cotangent_sixteen.reshape(128, 256), cotangent_coarse.reshape(32, 256),
        const(chunk_split()), const(column_pick()), const(ring_pick()), const(small_send()),
        const(small_taps()), const(quads), const(quads.transpose(0, 2, 1)), const(cot_pick()),
        const(rings[0]), const(rings[1]),
    )
    split4, split8 = (const(np.stack([interleave(n), interleave(n).T])) for n in (4, 2))
    out4, out8, dx = levels(
        xe, wo.reshape(640, 3584), wr.reshape(640, 3584), c2t, conv, cot4, cot8, ring4, ring8, dx_small,
        const(shift_matrices().reshape(9, TOK, TOK)), split4, split8,
        first_bias.reshape(1, 640), mid_gain.reshape(1, 640), mid_shift.reshape(1, 640),
        bias4, bias8, level_gain, level_shift,
    )
    grads, weight = last(dx, attn_t)
    return (
        out4.reshape(1, 64, 32, 256),
        out8.reshape(1, 32, 16, 256),
        lev16.reshape(1, 16, 8, 256),
        levc.reshape(1, 8, 4, 256),
        grads[None],
        weight,
    )


def solution(mesh):
    tokens = P("segment", ("tr", "tc"), None)
    deconv = P("segment", None, None, None)
    grid = P("segment", "tr", "tc", None)
    placed = (
        (tokens, tokens, deconv) + (P(),) * 5 + (deconv,) + (P(),) * 8 + (grid,) * 4
    )
    return jax.shard_map(
        body,
        mesh=mesh,
        in_specs=placed,
        out_specs=(grid, grid, grid, grid, tokens, P(("segment", "tr", "tc"), None)),
        check_vma=False,
    )
```

time: 608 us -> 145 us (0.24); the launches traced: 598 us -> 145 us
  waiting for transfers between devices: 220 us -> 0 us
  Pallas kernels: 0 us -> 132 us
  local copies, waits for them, and re-layouts: 141 us -> 12.1 us
  starting transfers between devices: 107 us -> 0 us
  matrix products: 64.4 us -> 0 us
  other arithmetic: 37.7 us -> 0 us
  between operations: 16.7 us -> 0.68 us
  blocking collectives: 11.7 us -> 0 us
    unnamed x4 -> x0, waiting for transfers between devices: 161 us -> none
    pallas_call x0 -> x3, Pallas kernels: none -> 132 us  [call(): pl.pallas_call(kernel, out_shape=outs, in_specs=[vmem] * len(args), out_s...]
    ppermute x34 -> x0, starting transfers between devices: 100 us -> none  [the longest x16 70 us: with_halo(): before = lax.ppermute(last, axis, up)]
    reshape x11 -> x7, local copies, waits for them, and re-layouts: 66.2 us -> 8.25 us  [the longest x1 1.33 us: body(): cotangent_coarse.reshape(32, 256)]
    dot_general x15 -> x0, matrix products: 41.1 us -> none  [the longest x6 27 us: expand_pixels(): jnp.dot(pixels.reshape(height * breadth, channels), weight.reshape(channe...]
    all_gather x2 -> x0, waiting for transfers between devices: 33.1 us -> none  [the longest x1 33.1 us: body(): lax.all_gather(first_deconv, 'segment', axis=0, tiled=True)]
    conv_general_dilated x8 -> x0, matrix products: 23.2 us -> none  [conv_three(): lax.conv_general_dilated(padded[None], kernel, (1, 1), 'VALID', dimension...]
    convert_element_type x12 -> x0, local copies, waits for them, and re-layouts: 20.6 us -> none  [the longest x2 7.4 us: lift_levels(): expand_pixels(upsampled, second_deconv, second_bias).astype(jnp.bfloat16)]
  transfers between devices with their start and end apart: 38 -> 0, of which waited for: 8 -> 0; matrix products, arithmetic and copies ran while one was open for 28% -> 0% of each run, Pallas kernels for 0% -> 0%
where the time goes in v1:
time: 145 us
  Pallas kernels  132 us (91%)
  local copies, waits for them, and re-layouts  12.1 us (8%)
    pallas_call x3, Pallas kernels, call(): pl.pallas_call(kernel, out_shape=outs, in_specs=[vmem] * len(args), out_s...  132 us
    unnamed x7, local copies, waits for them, and re-layouts  3.88 us

profile of v1, /device:TPU:1, one launch (start us, length us, event | category | flops | bytes accessed | tf_op | source)
XLA Modules:
  0.0 144.8 jit_solution(15520313008995052174)
XLA Ops:
  0.6 1.2 reshape.64.b2
  1.9 1.3 reshape.73.bias1
  3.1 1.3 reshape.74.gain_m
  4.4 1.3 reshape.75.shift_m
  5.7 1.3 reshape.65.bh
  6.9 1.3 reshape.70.cotc
  8.3 59.1 %shard_map.361 = (bf16[8,80,3584]{2,1,0:T(8,128)(2,1)}, bf16[8,80,3584]{2,1,0:T(8,128)(2,1)}, bf16[192,1280]{1,0:T(8,128)(2,1)}, bf16[4,256,640]{2,1,0:T(8,128)(...) custom-call(bf16[128,1280]{1,0:T(8,128)(2,1)} %bitcast.25, ...), custom_call_target="tpu_custom_call" | custom-call | tf_op jit(solution)/shard_map/pallas_call | solution.py:490
  67.4 0.0 copy-start.1
  67.4 0.0 copy-start
  67.4 34.9 %shard_map.362 = (bf16[16,4,32,256]{3,2,1,0:T(8,128)(2,1)}, bf16[16,2,16,256]{3,2,1,0:T(8,128)(2,1)}, bf16[128,1280]{1,0:T(8,128)(2,1)}) custom-call(bf16[192,1280]{1,0:T(8,128)(2,1)} %get-tuple-element.23.xe, bf16[640,3584]{1,0:T(8,128)(2,1)} %bitcast.17, bf16[640,3584]{1,0:T(8,128)(2,1)} %bitcast.18, bf16[4,256,640]{2,1,0:T(8,128)(2,1)} %get-tuple-element.26.second, ...), custom_call_target="tpu_custom_call" | custom-call | tf_op jit(solution)/shard_map/pallas_call | solution.py:490
  102.3 38.0 %shard_map.363 = (bf16[128,1280]{1,0:T(8,128)(2,1)}, f32[10,1280]{1,0:T(8,128)}) custom-call(bf16[128,1280]{1,0:T(8,128)(2,1)} %get-tuple-element.36.dx, bf16[256,1024]{1,0:T(8,128)(2,1)} %get-tuple-element.37.attn_t), custom_call_target="tpu_custom_call" | custom-call | tf_op jit(solution)/shard_map/pallas_call | solution.py:490
  140.3 0.0 copy-done.1
  140.3 0.6 reshape.79
  141.0 0.0 copy-done
  141.0 0.6 copy.43
  141.6 1.7 %copy.44 = bf16[1,128,1280]{2,1,0:T(8,128)(2,1)} copy(bf16[1,128,1280]{2,1,0:T(8,128)(2,1)} %bitcast.24) | data formatting | bytes 655360
  143.3 1.5 %copy.45 = f32[10,1280]{1,0:T(8,128)} copy(f32[10,1280]{1,0:T(8,128)} %get-tuple-element.51) | data formatting | bytes 102400
Async XLA Ops:
  67.4 73.0 %copy-start.1 = (bf16[32,256]{1,0:T(8,128)(2,1)S(1)}, bf16[32,256]{1,0:T(8,128)(2,1)}, u32[]{:S(2)}) copy-start(bf16[32,256]{1,0:T(8,128)(2,1)} %get-tuple-element.35) | copy-start | bytes 49156
  67.4 73.6 %copy-start = (bf16[128,256]{1,0:T(8,128)(2,1)S(1)}, bf16[128,256]{1,0:T(8,128)(2,1)}, u32[]{:S(2)}) copy-start(bf16[128,256]{1,0:T(8,128)(2,1)} %get-tuple-element.34) | copy-start | bytes 196612

commit v2 on v1

--- a/solution.py
+++ b/solution.py
@@ -277,7 +277,7 @@
             copy.wait_send()
 
 
-SPLIT = 1792
+SPLIT = 896
 
 
 def split_product(row, weight):
@@ -289,17 +289,21 @@
     return total
 
 
-def front_kernel(
+def main_kernel(
     feat, attn, first, half, k2t, l4, l8, l16, lc, b2, bh, conv, gains, offsets, cot4, cot8, cot16, cotc,
     split, columns, ring_sel, edges, taps, quad, quad_t, cot_sel, cot_ring4, cot_ring8,
-    wo, wr, xe, c2t, bias4, bias8, ring4, ring8, attn_t, dx_small, lev16, levc,
-    w_own, w_rem, xa, aa, xt, at, xh, sides, small, small_h, back, back_h, cotm, cot_h, attn_c, attn_h, send, recv,
+    shifts, split4, split8, bias1, gain_m, shift_m,
+    out4, out8, lev16, levc, home_out, parts_out,
+    w, first_v, half_v, xa, aa, xt, at, xh, sides, small, small_h, back_s, back_h, cotm, cot_h, attn_c, attn_h,
+    xe, c2t, ring4, ring8, dx_small, up, unit_u, slope_u, scale_u, lat, back, unit_l, scale_l, d4, dfull,
+    attn_t, mine, home, tiles, part, parts, send, recv, load,
 ):
     s, tr, tc = place()
     other = 1 - s
     x_hi, y, z, core = tr // 4, tr % 4, tc // 2, tc % 2
     turn = 1 - 2 * core
     far = (other, (1 - x_hi) * 4 + y, tc)
+    balance = (other, (1 - x_hi + core * (2 * x_hi - 1)) * 4 + y, tc)
     sibling = (s, tr, tc + turn)
     z_ahead = (s, tr, (z + turn + 4) % 4 * 2 + core)
     z_behind = (s, tr, (z - turn + 4) % 4 * 2 + core)
@@ -308,30 +312,68 @@
     around = [neighbour(k, s, tr, tc) for k in range(8)]
     across = [(other, tr, (tc + o) % 8) for o in range(8)]
     along = [(s, tr, (tc + o) % 8) for o in range(1, 8)]
-    peers = across + [far, sibling, z_ahead, z_behind, y_ahead, y_behind] + around + along
+    me = s * 8 + tr
+    plane = [((me + o) % 16 // 8, (me + o) % 8, tc) for o in range(1, 16)]
+    peers = plane + across + [far, balance, sibling, z_ahead, z_behind, y_ahead, y_behind] + around + along
     signal_all(peers)
     copies = Copies(send, recv)
 
-    def relayout(chunk):
-        rows = pl.ds(pl.multiple_of(chunk * 80, 80), 80)
-        block = mm(split[...], first[rows].reshape(320, 640)).astype(BF16)
-        product = mm(half[rows].reshape(320, 640), l8[...]).astype(BF16)
+    def chunk_at(i):
+        return i % 2 * 4 + (jnp.where(i % 2 == 0, z, y) + i // 2) % 4
+
+    def loads(slot):
+        rows = pl.ds(chunk_at(order[slot]) * 80, 80)
+        return [
+            pltpu.make_async_copy(ref.at[rows], slots.at[slot], load.at[k, slot])
+            for k, (ref, slots) in enumerate(((first, first_v), (half, half_v)))
+        ]
+
+    def relayout(slot):
+        for copy in loads(slot):
+            copy.wait()
+        block = mm(split[...], first_v[slot].reshape(320, 640)).astype(BF16)
+        product = mm(half_v[slot].reshape(320, 640), l8[...]).astype(BF16)
         product = mm(split[...], product).astype(BF16)
+        rows = pl.ds(pl.multiple_of(640 * s + chunk_at(order[slot]) * 80, 16), 80)
         for p in range(4):
-            w_own[chunk, :, 640 * p : 640 * p + 640] = block[80 * p : 80 * p + 80]
-            w_own[chunk, :, 2560 + 256 * p : 2816 + 256 * p] = product[80 * p : 80 * p + 80]
-
+            w[rows, 640 * p : 640 * p + 640] = block[80 * p : 80 * p + 80]
+            w[rows, 2560 + 256 * p : 2816 + 256 * p] = product[80 * p : 80 * p + 80]
+        return w.at[rows]
+
+    order = [0, 1, 2 + core, 4 + core, 6 + core]
+
+    def piece(owner, chunk, h):
+        rows = pl.ds(pl.multiple_of(640 * owner + chunk * 80, 16), 80)
+        return w.at[rows, pl.ds(pl.multiple_of(core * 2 * SPLIT + h * SPLIT, 128), SPLIT)]
+
+    def send_pieces(chunk, peer):
+        return [copies.start(piece(s, chunk, h), piece(s, chunk, h), peer) for h in range(2)]
+
+    shared = []
+
+    def pass_on(arrived, chunk, peers):
+        sent = [[] for _ in peers]
+        for h, copy in enumerate(arrived):
+            copy.wait_recv()
+            part = piece(other, chunk, h)
+            for onward, peer in zip(sent, peers):
+                onward.append(copies.start(part, part, peer))
+            shared.append(copies.start(part, part, sibling))
+        return sent
+
+    for slot in range(5):
+        for copy in loads(slot):
+            copy.start()
     for j in range(8):
         for i in range(2):
             xa[j, 8 * i : 8 * i + 8] = feat[64 * i + 8 * j : 64 * i + 8 * j + 8]
             aa[j, 8 * i : 8 * i + 8] = attn[64 * i + 8 * j : 64 * i + 8 * j + 8]
-    relayout(z)
+    relayout(0)
     wait_all(peers)
-    mine = pl.ds(pl.multiple_of(core * SPLIT, 128), SPLIT)
     x_copies = [copies.start(xa.at[(tc + o) % 8], xt.at[tc], across[o]) for o in range(8)]
-    z_first = copies.start(w_own.at[z, :, mine], w_rem.at[z, :, mine], far)
-    relayout(4 + y)
-    y_first = copies.start(w_own.at[4 + y, :, mine], w_rem.at[4 + y, :, mine], far)
+    z_first = send_pieces(z, far)
+    relayout(1)
+    y_first = send_pieces(4 + y, balance)
     pixels = jnp.concatenate([cot4[...].reshape(2048, 256), cot8[...].reshape(512, 256)])
     cotm[...] = pick(cot_sel[...], pixels)
     cot_copies = [
@@ -343,15 +385,10 @@
         for k in range(8)
     ]
 
-    @pl.loop(1, 4)
-    def rest(i):
-        relayout((z + i) % 4)
-        relayout(4 + (y + i) % 4)
-
-    shared = []
-
-    def share(chunk):
-        shared.append(copies.start(w_rem.at[chunk, :, mine], w_rem.at[chunk, :, mine], sibling))
+    for slot in range(2, 5):
+        rows = relayout(slot)
+        shared.append(copies.start(rows, rows, sibling))
+    z_up, z_down = pass_on(z_first, z, [z_ahead, z_behind])
 
     for copy in x_copies:
         copy.wait_recv()
@@ -387,21 +424,14 @@
         return sums
 
     small_copies = exchange(laterals, small, small_h)
-    z_first.wait_recv()
-    z_up = copies.start(w_rem.at[z, :, mine], w_rem.at[z, :, mine], z_ahead)
-    z_down = copies.start(w_rem.at[z, :, mine], w_rem.at[z, :, mine], z_behind)
-    share(z)
-    a_copies = [copies.start(aa.at[(tc + o) % 8], at.at[tc], across[o]) for o in range(8)]
     for p in range(4):
         c2t[p] = lax.dot_general(
             l4[...], k2t[p], (((0,), (0,)), ((), ())), preferred_element_type=F32
         ).astype(BF16)
-    bias4[...] = split_product(b2[...], l4[...])
-    bias8[...] = split_product(bh[...], l8[...])
-    y_first.wait_recv()
-    y_up = copies.start(w_rem.at[4 + y, :, mine], w_rem.at[4 + y, :, mine], y_ahead)
-    y_down = copies.start(w_rem.at[4 + y, :, mine], w_rem.at[4 + y, :, mine], y_behind)
-    share(4 + y)
+    bias4 = split_product(b2[...].reshape(1, 320), l4[...])
+    bias8 = split_product(bh[...].reshape(1, 640), l8[...])
+    y_up, y_down = pass_on(y_first, 4 + y, [y_ahead, y_behind])
+    a_copies = [copies.start(aa.at[(tc + o) % 8], at.at[tc], across[o]) for o in range(8)]
     for copy in small_copies:
         copy.wait_recv()
     sums = small_conv(laterals, small_h, mm, lambda t: t)
@@ -409,23 +439,17 @@
     for i, (cot, level_out) in enumerate(((cot16, lev16), (cotc, levc))):
         unit, scale = normed(sums[i])
         gain = gains[2 + i, 1:2]
-        level_out[...] = (unit * gain + offsets[2 + i, 1:2]).astype(BF16)
-        grads.append(norm_back(unit, scale, cot[...].astype(F32) * gain).astype(BF16))
+        level_out[...] = (unit * gain + offsets[2 + i, 1:2]).astype(BF16).reshape(level_out.shape)
+        grads.append(norm_back(unit, scale, cot[...].reshape(-1, 256).astype(F32) * gain).astype(BF16))
     grads = jnp.concatenate(grads)
-    back_copies = exchange(grads, back, back_h)
+    back_copies = exchange(grads, back_s, back_h)
 
     z_ring = [(z - turn + 4) % 4, (z + turn + 4) % 4, (z + 2) % 4]
     y_ring = [4 + (y - turn + 4) % 4, 4 + (y + turn + 4) % 4, 4 + (y + 2) % 4]
-    z_up.wait_recv()
-    z_on = copies.start(w_rem.at[z_ring[0], :, mine], w_rem.at[z_ring[0], :, mine], z_ahead)
-    share(z_ring[0])
-    z_down.wait_recv()
-    share(z_ring[1])
-    y_up.wait_recv()
-    y_on = copies.start(w_rem.at[y_ring[0], :, mine], w_rem.at[y_ring[0], :, mine], y_ahead)
-    share(y_ring[0])
-    y_down.wait_recv()
-    share(y_ring[1])
+    (z_on,) = pass_on(z_up, z_ring[0], [z_ahead])
+    (y_on,) = pass_on(y_up, y_ring[0], [y_ahead])
+    pass_on(z_down, z_ring[1], [])
+    pass_on(y_down, y_ring[1], [])
 
     for copy in a_copies:
         copy.wait_recv()
@@ -463,18 +487,106 @@
     xe[OWN:] = pick(ring_sel[...], xh[...].reshape(128, 1280))
     ring4[...] = pick(cot_ring4[...], cot_h[...]).reshape(4, 4, RING, 256)
     ring8[...] = pick(cot_ring8[...], cot_h[...]).reshape(2, 2, RING, 256)
-    wo[...] = w_own[...]
-    z_on.wait_recv()
-    share(z_ring[2])
-    y_on.wait_recv()
-    share(y_ring[2])
+    pass_on(z_on, z_ring[2], [])
+    pass_on(y_on, y_ring[2], [])
+    for copy in shared:
+        copy.wait_recv()
+    keep = exists_mask(TOK, RING_SPANS)
+    bias1, gain_m, shift_m = (ref[...].reshape(1, 640) for ref in (bias1, gain_m, shift_m))
+    for p in range(4):
+        cols = pl.ds(640 * p, 640)
+        pre = mm(xe[...], w[:, cols]) + bias1
+        unit, size = normed(pre)
+        before = unit * gain_m + shift_m
+        cdf = 0.5 * (1 + erf(before * (0.5**0.5)))
+        up[p] = (before * cdf).astype(BF16)
+        inner = before[:OWN]
+        unit_u[p] = unit[:OWN]
+        scale_u[p] = size[:OWN]
+        slope_u[p] = (cdf[:OWN] + inner * jnp.exp(-0.5 * inner * inner) * (1 / np.sqrt(2 * np.pi))) * gain_m
+    for p in range(4):
+        for q in range(4):
+            ph, pw = 2 * (p // 2) + q // 2, 2 * (p % 2) + q % 2
+            pre = mt(up[p], c2t[q]) + bias4
+            unit, size = normed(pre)
+            unit_l[ph, pw] = unit[:OWN]
+            scale_l[ph, pw] = size[:OWN]
+            lat[ph + 1, pw + 1] = ((unit * gains[0, 0:1] + offsets[0, 0:1]) * keep).astype(BF16)
+    def done4(ph, pw, grads):
+        d4[2 * (ph // 2) + pw // 2, 2 * (ph % 2) + pw % 2] = grads
+
+    def done8(ph, pw, grads):
+        d8[2 * ph + pw] = grads
+
+    d8 = d4.at[4]
+    pyramid_level(
+        4, lat, back, unit_l, scale_l, conv.at[0], cot4, ring4, out4, gains[0], offsets[0], keep, shifts, split4, done4
+    )
+    for p in range(4):
+        cols = pl.ds(2560 + 256 * p, 256)
+        pre = mm(xe[...], w[:, cols]) + bias8
+        unit, size = normed(pre)
+        unit_l[p // 2, p % 2] = unit[:OWN]
+        scale_l[p // 2, p % 2] = size[:OWN]
+        lat[p // 2 + 1, p % 2 + 1] = ((unit * gains[1, 0:1] + offsets[1, 0:1]) * keep).astype(BF16)
+
+    pyramid_level(
+        2, lat, back, unit_l, scale_l, conv.at[1], cot8, ring8, out8, gains[1], offsets[1], keep, shifts, split8, done8
+    )
+    dup = jnp.zeros((4 * OWN, 640), F32)
+    for q in range(4):
+        block = jnp.concatenate([d4[p, q] for p in range(4)], axis=0)
+        dup = dup + mm(block, c2t[q])
+    for p in range(4):
+        grads = norm_back(unit_u[p], scale_u[p], dup[p * OWN : p * OWN + OWN] * slope_u[p])
+        dfull[:, 640 * p : 640 * p + 640] = grads.astype(BF16)
+        dfull[:, 2560 + 256 * p : 2816 + 256 * p] = d4[4, p]
+    block_at = [tc, (tc - 2 * turn + 8) % 8, (tc + 2 * turn + 8) % 8, (tc + 4) % 8]
+    twins = [[], []]
+
+    def forward_tile(h, slot, peers):
+        block = tiles.at[h, slot]
+        twins[h].append(copies.start(block, block, sibling))
+        return [copies.start(block, block, peer) for peer in peers]
+
+    rings, homes = [], []
+    for h in range(2):
+        cols = pl.ds(640 * h, 640)
+        grads = (mt(dfull[...], w[cols]) + dx_small[:, cols]).astype(BF16).reshape(8, 16, 640)
+        mine[h] = grads
+        block = tiles.at[h, tc]
+        rings.append([copies.start(mine.at[h], block, peer) for peer in (z_ahead, z_behind)])
+        twins[h].append(copies.start(mine.at[h], block, sibling))
+        homes += [copies.start(mine.at[h, (tc + o) % 8], home.at[h, tc], across[o]) for o in range(8)]
+        tiles[h, tc] = grads
     for copy in attn_copies:
         copy.wait_recv()
     for j in range(8):
         attn_t[:, 128 * j : 128 * j + 128] = attn_h[j].T
-    for copy in shared:
+    onward = []
+    for h in range(2):
+        rings[h][0].wait_recv()
+        onward += forward_tile(h, block_at[1], [z_ahead])
+    sums = []
+    for h in range(2):
+        rings[h][1].wait_recv()
+        forward_tile(h, block_at[2], [])
+        onward[h].wait_recv()
+        forward_tile(h, block_at[3], [])
+        for copy in twins[h]:
+            copy.wait_recv()
+        product = mm(attn_t[...], tiles[h].reshape(8 * OWN, 640))
+        part[h] = product.astype(BF16).reshape(16, 16, 640)
+        sums += [
+            copies.start(part.at[h, (me + o) % 16], parts.at[h, me], plane[o - 1]) for o in range(1, 16)
+        ]
+        parts[h, me] = part[h, me]
+    for copy in homes:
         copy.wait_recv()
-    wr[...] = w_rem[...]
+    home_out[...] = home[...]
+    for copy in sums:
+        copy.wait_recv()
+    parts_out[...] = parts[...]
     copies.finish()
 
 
@@ -482,15 +594,15 @@
     return jax.ShapeDtypeStruct(dims, dtype)
 
 
-def call(kernel, outs, scratch, args, collective_id=None):
+def call(kernel, outs, scratch, args, collective_id=None, specs=None):
     vmem = pl.BlockSpec(memory_space=pltpu.VMEM)
-    params = {"vmem_limit_bytes": 60 * 2**20}
+    params = {"vmem_limit_bytes": 62 * 2**20}
     if collective_id is not None:
         params.update(collective_id=collective_id, has_side_effects=True)
     return pl.pallas_call(
         kernel,
         out_shape=outs,
-        in_specs=[vmem] * len(args),
+        in_specs=specs or [vmem] * len(args),
         out_specs=[vmem] * len(outs),
         scratch_shapes=scratch,
         compiler_params=pltpu.CompilerParams(**params),
@@ -499,28 +611,6 @@
 
 def buffer(*dims):
     return pltpu.VMEM(dims, BF16)
-
-
-def front(*args):
-    copies = 8 + 2 + 8 + 8 + 8 + 4 + 8 + 8 + 8 + 2 + 7
-    return call(
-        front_kernel,
-        [
-            shape((8, 80, 3584)), shape((8, 80, 3584)), shape((TOK, 1280)), shape((4, 256, 640)),
-            shape((1, 256), F32), shape((1, 256), F32), shape((4, 4, RING, 256)), shape((2, 2, RING, 256)),
-            shape((256, 1024)), shape((OWN, 1280), F32), shape((128, 256)), shape((32, 256)),
-        ],
-        [
-            buffer(8, 80, 3584), buffer(8, 80, 3584),
-            buffer(8, 16, 1280), buffer(8, 16, 1280), buffer(8, 16, 1280), buffer(8, 16, 1280),
-            buffer(8, 16, 1280), buffer(2, 16, 1280),
-            buffer(SMALL, 256), buffer(SMALL, 256), buffer(SMALL, 256), buffer(SMALL, 256),
-            buffer(COT, 256), buffer(COT, 256), buffer(8, OWN, 256), buffer(8, OWN, 256),
-            pltpu.SemaphoreType.DMA((copies,)), pltpu.SemaphoreType.DMA((copies,)),
-        ],
-        args,
-        collective_id=0,
-    )
 
 
 def erf(x):
@@ -589,138 +679,61 @@
             done(ph, pw, norm_back(unit[ph, pw], scale[ph, pw], grads).astype(BF16))
 
 
-def levels_kernel(
-    xe, wo, wr, second, conv, cot4, cot8, ring4, ring8, dx_small, shifts, split4, split8,
-    bias1, gain_m, shift_m, bias4, bias8, gains, offsets,
-    out4, out8, dx,
-    up, unit_u, slope_u, scale_u, lat4, back4, unit4, scale4, lat8, back8, unit8, scale8, d4, dfull,
-):
-    keep = exists_mask(TOK, RING_SPANS)
-    s, _, _ = place()
-    own = pl.ds(pl.multiple_of(640 * s, 128), 640)
-    other = pl.ds(pl.multiple_of(640 - 640 * s, 128), 640)
-    xo, xr = xe[:, own], xe[:, other]
-    for p in range(4):
-        cols = pl.ds(640 * p, 640)
-        pre = mm(xo, wo[:, cols]) + mm(xr, wr[:, cols]) + bias1[...]
-        unit, size = normed(pre)
-        before = unit * gain_m[...] + shift_m[...]
-        cdf = 0.5 * (1 + erf(before * (0.5**0.5)))
-        up[p] = (before * cdf).astype(BF16)
-        inner = before[:OWN]
-        unit_u[p] = unit[:OWN]
-        scale_u[p] = size[:OWN]
-        slope_u[p] = (cdf[:OWN] + inner * jnp.exp(-0.5 * inner * inner) * (1 / np.sqrt(2 * np.pi))) * gain_m[...]
-    for p in range(4):
-        for q in range(4):
-            ph, pw = 2 * (p // 2) + q // 2, 2 * (p % 2) + q % 2
-            pre = mt(up[p], second[q]) + bias4[...]
-            unit, size = normed(pre)
-            unit4[ph, pw] = unit[:OWN]
-            scale4[ph, pw] = size[:OWN]
-            lat4[ph + 1, pw + 1] = ((unit * gains[0, 0:1] + offsets[0, 0:1]) * keep).astype(BF16)
-    for p in range(4):
-        cols = pl.ds(2560 + 256 * p, 256)
-        pre = mm(xo, wo[:, cols]) + mm(xr, wr[:, cols]) + bias8[...]
-        unit, size = normed(pre)
-        unit8[p // 2, p % 2] = unit[:OWN]
-        scale8[p // 2, p % 2] = size[:OWN]
-        lat8[p // 2 + 1, p % 2 + 1] = ((unit * gains[1, 0:1] + offsets[1, 0:1]) * keep).astype(BF16)
-
-    def done4(ph, pw, grads):
-        d4[2 * (ph // 2) + pw // 2, 2 * (ph % 2) + pw % 2] = grads
-
-    def done8(ph, pw, grads):
-        d8[2 * ph + pw] = grads
-
-    d8 = d4.at[4]
-    pyramid_level(
-        4, lat4, back4, unit4, scale4, conv.at[0], cot4, ring4, out4, gains[0], offsets[0], keep, shifts, split4, done4
-    )
-    pyramid_level(
-        2, lat8, back8, unit8, scale8, conv.at[1], cot8, ring8, out8, gains[1], offsets[1], keep, shifts, split8, done8
-    )
-    dup = jnp.zeros((4 * OWN, 640), F32)
-    for q in range(4):
-        block = jnp.concatenate([d4[p, q] for p in range(4)], axis=0)
-        dup = dup + mm(block, second[q])
-    for p in range(4):
-        grads = norm_back(unit_u[p], scale_u[p], dup[p * OWN : p * OWN + OWN] * slope_u[p])
-        dfull[:, 640 * p : 640 * p + 640] = grads.astype(BF16)
-        dfull[:, 2560 + 256 * p : 2816 + 256 * p] = d4[4, p]
-    dx[:, own] = (mt(dfull[...], wo[...]) + dx_small[:, own]).astype(BF16)
-    dx[:, other] = (mt(dfull[...], wr[...]) + dx_small[:, other]).astype(BF16)
-
-
-def levels(*args):
+def main(*args):
     def wide(*dims):
         return pltpu.VMEM(dims, F32)
 
+    vmem, anywhere = pl.BlockSpec(memory_space=pltpu.VMEM), pl.BlockSpec(memory_space=pl.ANY)
+    specs = [anywhere if i in (2, 3) else vmem for i in range(len(args))]
+    copies = 8 + 4 + 8 + 8 + 8 + 8 + 8 + 8 + 4 + 16 + 3 + 7 + 2 * (2 + 1 + 8 + 1 + 3 + 15)
     return call(
-        levels_kernel,
-        [shape((16, 4, 32, 256)), shape((16, 2, 16, 256)), shape((OWN, 1280))],
+        main_kernel,
         [
-            buffer(4, TOK, 640), wide(4, OWN, 640), wide(4, OWN, 640), wide(4, OWN, 1),
+            shape((16, 4, 32, 256)), shape((16, 2, 16, 256)), shape((16, 8, 256)), shape((8, 4, 256)),
+            shape((2, 8, 16, 640)), shape((2, 16, 16, 640)),
+        ],
+        [
+            buffer(1280, 3584), buffer(5, 80, 2, 2, 640), buffer(5, 80, 2, 2, 640),
+            buffer(8, 16, 1280), buffer(8, 16, 1280), buffer(8, 16, 1280), buffer(8, 16, 1280),
+            buffer(8, 16, 1280), buffer(2, 16, 1280),
+            buffer(SMALL, 256), buffer(SMALL, 256), buffer(SMALL, 256), buffer(SMALL, 256),
+            buffer(COT, 256), buffer(COT, 256), buffer(8, OWN, 256), buffer(8, OWN, 256),
+            buffer(TOK, 1280), buffer(4, 256, 640), buffer(4, 4, RING, 256), buffer(2, 2, RING, 256),
+            wide(OWN, 1280), buffer(4, TOK, 640), wide(4, OWN, 640), wide(4, OWN, 640), wide(4, OWN, 1),
             buffer(6, 6, TOK, 256), buffer(6, 6, TOK, 256), wide(4, 4, OWN, 256), wide(4, 4, OWN, 1),
-            buffer(4, 4, TOK, 256), buffer(4, 4, TOK, 256), wide(2, 2, OWN, 256), wide(2, 2, OWN, 1),
-            buffer(5, 4, OWN, 256), buffer(OWN, 3584),
+            buffer(5, 4, OWN, 256), buffer(OWN, 3584), buffer(256, 1024),
+            buffer(2, 8, 16, 640), buffer(2, 8, 16, 640), buffer(2, 8, 8, 16, 640),
+            buffer(2, 16, 16, 640), buffer(2, 16, 16, 640),
+            pltpu.SemaphoreType.DMA((copies,)), pltpu.SemaphoreType.DMA((copies,)),
+            pltpu.SemaphoreType.DMA((2, 5)),
         ],
         args,
-    )
-
-
-def last_kernel(dx, attn_t, grads, weight, mine, home, tiles, part, parts, send, recv):
-    s, tr, tc = place()
-    other, me = 1 - s, s * 8 + tr
-    sibling = (s, tr, tc + 1 - 2 * (tc % 2))
-    ring = [(s, tr, (tc + 2 * j) % 8) for j in (1, 3, 2)]
-    across = [(other, tr, (tc + o) % 8) for o in range(8)]
-    plane = [((me + o) % 16 // 8, (me + o) % 8, tc) for o in range(1, 16)]
-    peers = across + ring + [sibling] + plane
-    signal_all(peers)
-    copies = Copies(send, recv)
-    mine[...] = dx[...].reshape(8, 16, 1280)
-    wait_all(peers)
-    received = [copies.start(mine, tiles.at[tc], peer) for peer in ring]
-    shared = [copies.start(mine, tiles.at[tc], sibling)]
-    homes = [copies.start(mine.at[(tc + o) % 8], home.at[tc], across[o]) for o in range(8)]
-    tiles[tc] = mine[...]
-    for copy, j in zip(received, (1, 3, 2)):
-        copy.wait_recv()
-        slot = (tc + 8 - 2 * j) % 8
-        shared.append(copies.start(tiles.at[slot], tiles.at[slot], sibling))
-    for copy in shared:
-        copy.wait_recv()
-    product = mm(attn_t[...], tiles[...].reshape(8 * OWN, 1280))
-    part[...] = product.astype(BF16).reshape(16, 16, 1280)
-    sums = [copies.start(part.at[(me + o) % 16], parts.at[me], plane[o - 1]) for o in range(1, 16)]
-    parts[me] = part[me]
-    for copy in homes:
-        copy.wait_recv()
-    for j in range(8):
-        for i in range(2):
-            grads[64 * i + 8 * j : 64 * i + 8 * j + 8] = home[j, 8 * i : 8 * i + 8]
-    for copy in sums:
-        copy.wait_recv()
-    total = parts[0].astype(F32)
-    for j in range(1, 16):
-        total = total + parts[j].astype(F32)
-    weight[...] = total[:10]
-    copies.finish()
-
-
-def last(*args):
-    copies = 3 + 1 + 8 + 3 + 15
+        collective_id=0,
+        specs=specs,
+    )
+
+
+def finish_kernel(home, parts, *levels_and_outs):
+    ins, (grads, weight), outs = levels_and_outs[:4], levels_and_outs[4:6], levels_and_outs[6:]
+    for h in range(2):
+        cols = slice(640 * h, 640 * h + 640)
+        for j in range(8):
+            for i in range(2):
+                grads[64 * i + 8 * j : 64 * i + 8 * j + 8, cols] = home[h, j, 8 * i : 8 * i + 8]
+        total = parts[h, 0].astype(F32)
+        for j in range(1, 16):
+            total = total + parts[h, j].astype(F32)
+        weight[:, cols] = total[:10]
+    for level_in, level_out in zip(ins, outs):
+        level_out[...] = level_in[...]
+
+
+def finish(home, parts, *levels):
     return call(
-        last_kernel,
-        [shape((OWN, 1280)), shape((10, 1280), F32)],
-        [
-            buffer(8, 16, 1280), buffer(8, 16, 1280), buffer(8, 8, 16, 1280),
-            buffer(16, 16, 1280), buffer(16, 16, 1280),
-            pltpu.SemaphoreType.DMA((copies,)), pltpu.SemaphoreType.DMA((copies,)),
-        ],
-        args,
-        collective_id=1,
+        finish_kernel,
+        [shape((OWN, 1280)), shape((10, 1280), F32)] + [shape(level.shape) for level in levels],
+        [],
+        (home, parts) + levels,
     )
 
 
@@ -753,29 +766,23 @@
     cot8 = cotangent_eight.reshape(16, 2, 16, 256)
     quads = quad_pick()
     rings = cot_ring(4), cot_ring(2)
-    wo, wr, xe, c2t, bias4, bias8, ring4, ring8, attn_t, dx_small, lev16, levc = front(
+    split4, split8 = (const(np.stack([interleave(n), interleave(n).T])) for n in (4, 2))
+    out4, out8, lev16, levc, home, parts = main(
         features[0], attn_hidden[0], first_deconv, half_deconv, k2t,
-        lateral_four, lateral_eight, lateral_sixteen, lateral_coarse,
-        second_bias.reshape(1, 320), half_bias.reshape(1, 640),
-        conv, level_gain, level_shift, cot4, cot8,
-        cotangent_sixteen.reshape(128, 256), cotangent_coarse.reshape(32, 256),
+        lateral_four, lateral_eight, lateral_sixteen, lateral_coarse, second_bias, half_bias,
+        conv, level_gain, level_shift, cot4, cot8, cotangent_sixteen[0], cotangent_coarse[0],
         const(chunk_split()), const(column_pick()), const(ring_pick()), const(small_send()),
         const(small_taps()), const(quads), const(quads.transpose(0, 2, 1)), const(cot_pick()),
         const(rings[0]), const(rings[1]),
-    )
-    split4, split8 = (const(np.stack([interleave(n), interleave(n).T])) for n in (4, 2))
-    out4, out8, dx = levels(
-        xe, wo.reshape(640, 3584), wr.reshape(640, 3584), c2t, conv, cot4, cot8, ring4, ring8, dx_small,
         const(shift_matrices().reshape(9, TOK, TOK)), split4, split8,
-        first_bias.reshape(1, 640), mid_gain.reshape(1, 640), mid_shift.reshape(1, 640),
-        bias4, bias8, level_gain, level_shift,
-    )
-    grads, weight = last(dx, attn_t)
+        first_bias, mid_gain, mid_shift,
+    )
+    grads, weight, out4, out8, lev16, levc = finish(home, parts, out4, out8, lev16, levc)
     return (
         out4.reshape(1, 64, 32, 256),
         out8.reshape(1, 32, 16, 256),
-        lev16.reshape(1, 16, 8, 256),
-        levc.reshape(1, 8, 4, 256),
+        lev16[None],
+        levc[None],
         grads[None],
         weight,
     )

time: 145 us -> 108 us (0.74)
  Pallas kernels: 132 us -> 107 us
  local copies, waits for them, and re-layouts: 12.1 us -> 0 us
    pallas_call x3 -> x2, Pallas kernels: 132 us -> 107 us  [call(): pl.pallas_call(kernel, out_shape=outs, in_specs=specs or [vmem] * len(arg...]
    reshape x7 -> x0, local copies, waits for them, and re-layouts: 8.25 us -> none  [the longest x1 1.33 us: body(): cotangent_coarse.reshape(32, 256)]
    unnamed x7 -> x0, local copies, waits for them, and re-layouts: 3.88 us -> none
where the time goes in v2:
time: 108 us; the launch traced here: 107 us
  Pallas kernels  107 us (99%)
    pallas_call x2, Pallas kernels, call(): pl.pallas_call(kernel, out_shape=outs, in_specs=specs or [vmem] * len(arg...  107 us

profile of v2, /device:TPU:1, one launch (start us, length us, event | category | flops | bytes accessed | tf_op | source)
XLA Modules:
  0.0 107.4 jit_solution(9800170785898744243)
XLA Ops:
  0.6 103.9 %shard_map.361 = (bf16[16,4,32,256]{3,2,1,0:T(8,128)(2,1)}, bf16[16,2,16,256]{3,2,1,0:T(8,128)(2,1)}, bf16[16,8,256]{2,1,0:T(8,128)(2,1)}, bf16[8,4,256]{2,1,0:T...) custom-call(bf16[128,1280]{1,0:T(8,128)(2,1)} %bitcast.18, bf16[128,1280]{1,0:T(8,128)(2,1)} %bitcast.19, ...), custom_call_target="tpu_custom_call" | custom-call | tf_op jit(solution)/shard_map/pallas_call | solution.py:602
  104.5 2.9 %shard_map.362 = (bf16[128,1280]{1,0:T(8,128)(2,1)}, f32[10,1280]{1,0:T(8,128)}, bf16[16,4,32,256]{3,2,1,0:T(8,128)(2,1)}, bf16[16,2,16,256]{3,2,1,0:T(8,128)(2,...) custom-call(bf16[2,8,16,640]{3,2,1,0:T(8,128)(2,1)} %get-tuple-element.18.home, ...), custom_call_target="tpu_custom_call" | custom-call | tf_op jit(solution)/shard_map/pallas_call | solution.py:602

commit v3 on v2

--- a/solution.py
+++ b/solution.py
@@ -277,9 +277,6 @@
             copy.wait_send()
 
 
-SPLIT = 896
-
-
 def split_product(row, weight):
     total = 0.0
     for _ in range(3):
@@ -294,9 +291,9 @@
     split, columns, ring_sel, edges, taps, quad, quad_t, cot_sel, cot_ring4, cot_ring8,
     shifts, split4, split8, bias1, gain_m, shift_m,
     out4, out8, lev16, levc, home_out, parts_out,
-    w, first_v, half_v, xa, aa, xt, at, xh, sides, small, small_h, back_s, back_h, cotm, cot_h, attn_c, attn_h,
+    w, first_v, half_v, xa, aa, xt, xh, sides, small, small_h, back_s, back_h, cotm, cot_h, attn_c, attn_h,
     xe, c2t, ring4, ring8, dx_small, up, unit_u, slope_u, scale_u, lat, back, unit_l, scale_l, d4, dfull,
-    attn_t, mine, home, tiles, part, parts, send, recv, load,
+    res4, res8, attn_t, mine, home, tiles, part, parts, send, recv, load,
 ):
     s, tr, tc = place()
     other = 1 - s
@@ -311,10 +308,9 @@
     y_behind = (s, x_hi * 4 + (y - turn + 4) % 4, tc)
     around = [neighbour(k, s, tr, tc) for k in range(8)]
     across = [(other, tr, (tc + o) % 8) for o in range(8)]
-    along = [(s, tr, (tc + o) % 8) for o in range(1, 8)]
     me = s * 8 + tr
     plane = [((me + o) % 16 // 8, (me + o) % 8, tc) for o in range(1, 16)]
-    peers = plane + across + [far, balance, sibling, z_ahead, z_behind, y_ahead, y_behind] + around + along
+    peers = plane + across[1:] + around[2:] + [z_ahead, z_behind]
     signal_all(peers)
     copies = Copies(send, recv)
 
@@ -324,15 +320,15 @@
     def loads(slot):
         rows = pl.ds(chunk_at(order[slot]) * 80, 80)
         return [
-            pltpu.make_async_copy(ref.at[rows], slots.at[slot], load.at[k, slot])
+            pltpu.make_async_copy(ref.at[rows], slots.at[slot % 4], load.at[k, slot % 4])
             for k, (ref, slots) in enumerate(((first, first_v), (half, half_v)))
         ]
 
     def relayout(slot):
         for copy in loads(slot):
             copy.wait()
-        block = mm(split[...], first_v[slot].reshape(320, 640)).astype(BF16)
-        product = mm(half_v[slot].reshape(320, 640), l8[...]).astype(BF16)
+        block = mm(split[...], first_v[slot % 4].reshape(320, 640)).astype(BF16)
+        product = mm(half_v[slot % 4].reshape(320, 640), l8[...]).astype(BF16)
         product = mm(split[...], product).astype(BF16)
         rows = pl.ds(pl.multiple_of(640 * s + chunk_at(order[slot]) * 80, 16), 80)
         for p in range(4):
@@ -344,24 +340,42 @@
 
     def piece(owner, chunk, h):
         rows = pl.ds(pl.multiple_of(640 * owner + chunk * 80, 16), 80)
-        return w.at[rows, pl.ds(pl.multiple_of(core * 2 * SPLIT + h * SPLIT, 128), SPLIT)]
-
-    def send_pieces(chunk, peer):
-        return [copies.start(piece(s, chunk, h), piece(s, chunk, h), peer) for h in range(2)]
-
-    shared = []
-
-    def pass_on(arrived, chunk, peers):
-        sent = [[] for _ in peers]
-        for h, copy in enumerate(arrived):
-            copy.wait_recv()
-            part = piece(other, chunk, h)
-            for onward, peer in zip(sent, peers):
-                onward.append(copies.start(part, part, peer))
-            shared.append(copies.start(part, part, sibling))
+        start, width = ((2560 + 512 * core, 512), (1280 * core, 1280))[h]
+        return w.at[rows, pl.ds(pl.multiple_of(start, 128), width)]
+
+    shared = [[], []]
+
+    def send_piece(h, chunk, peer, owner):
+        part = piece(owner, chunk, h)
+        return copies.start(part, part, peer)
+
+    def pass_on(h, arrived, chunk, peers):
+        arrived.wait_recv()
+        sent = [send_piece(h, chunk, peer, other) for peer in peers]
+        shared[h].append(send_piece(h, chunk, sibling, other))
         return sent
 
-    for slot in range(5):
+    z_ring = [(z - turn + 4) % 4, (z + turn + 4) % 4, (z + 2) % 4]
+    y_ring = [4 + (y - turn + 4) % 4, 4 + (y + turn + 4) % 4, 4 + (y + 2) % 4]
+    z_hops, y_hops = [None, None], [None, None]
+
+    def first_hop_z(h):
+        z_hops[h] = pass_on(h, z_first[h], z, [z_ahead, z_behind])
+
+    def first_hop_y(h):
+        y_hops[h] = pass_on(h, y_first[h], 4 + y, [y_ahead, y_behind])
+
+    def second_hop(h):
+        for hops, ring, ahead in ((z_hops, z_ring, z_ahead), (y_hops, y_ring, y_ahead)):
+            up, down = hops[h]
+            hops[h] = pass_on(h, up, ring[0], [ahead])
+            pass_on(h, down, ring[1], [])
+
+    def third_hop(h):
+        for hops, ring in ((z_hops, z_ring), (y_hops, y_ring)):
+            pass_on(h, hops[h][0], ring[2], [])
+
+    for slot in range(4):
         for copy in loads(slot):
             copy.start()
     for j in range(8):
@@ -369,11 +383,14 @@
             xa[j, 8 * i : 8 * i + 8] = feat[64 * i + 8 * j : 64 * i + 8 * j + 8]
             aa[j, 8 * i : 8 * i + 8] = attn[64 * i + 8 * j : 64 * i + 8 * j + 8]
     relayout(0)
+    for copy in loads(4):
+        copy.start()
     wait_all(peers)
+    z_first = [send_piece(0, z, far, s)]
     x_copies = [copies.start(xa.at[(tc + o) % 8], xt.at[tc], across[o]) for o in range(8)]
-    z_first = send_pieces(z, far)
+    z_first.append(send_piece(1, z, far, s))
     relayout(1)
-    y_first = send_pieces(4 + y, balance)
+    y_first = [send_piece(h, 4 + y, balance, s) for h in range(2)]
     pixels = jnp.concatenate([cot4[...].reshape(2048, 256), cot8[...].reshape(512, 256)])
     cotm[...] = pick(cot_sel[...], pixels)
     cot_copies = [
@@ -384,11 +401,32 @@
         )
         for k in range(8)
     ]
-
     for slot in range(2, 5):
         rows = relayout(slot)
-        shared.append(copies.start(rows, rows, sibling))
-    z_up, z_down = pass_on(z_first, z, [z_ahead, z_behind])
+        shared[0].append(copies.start(rows, rows, sibling))
+    first_hop_z(0)
+    first_hop_y(0)
+    tile = aa[...].reshape(OWN, 1280)
+    row = lax.broadcasted_iota(jnp.int32, (1280, 256), 0)
+    column = lax.broadcasted_iota(jnp.int32, (1280, 256), 1)
+    row = jnp.where(column % 16 < 10, row - column // 16 * 80 - column % 16, -1)
+
+    @pl.loop(0, 8)
+    def attn_columns(j):
+        attn_c[j] = mm(tile, (row == 10 * j).astype(F32).astype(BF16)).astype(BF16).reshape(8, 16, 256)
+
+    for p in range(4):
+        c2t[p] = lax.dot_general(
+            l4[...], k2t[p], (((0,), (0,)), ((), ())), preferred_element_type=F32
+        ).astype(BF16)
+    bias4 = split_product(b2[...].reshape(1, 320), l4[...])
+    bias8 = split_product(bh[...].reshape(1, 640), l8[...])
+    for copy in cot_copies:
+        copy.wait_recv()
+    ring4[...] = pick(cot_ring4[...], cot_h[...]).reshape(4, 4, RING, 256)
+    ring8[...] = pick(cot_ring8[...], cot_h[...]).reshape(2, 2, RING, 256)
+    second_hop(0)
+    first_hop_z(1)
 
     for copy in x_copies:
         copy.wait_recv()
@@ -424,14 +462,33 @@
         return sums
 
     small_copies = exchange(laterals, small, small_h)
+    first_hop_y(1)
+    third_hop(0)
+    for copy in halo_copies:
+        copy.wait_recv()
+    xe[:OWN] = x
+    xe[OWN:] = pick(ring_sel[...], xh[...].reshape(128, 1280))
+    for copy in shared[0]:
+        copy.wait_recv()
+    keep = exists_mask(TOK, RING_SPANS)
+
+    def done8(ph, pw, grads):
+        d8[2 * ph + pw] = grads
+
+    d8 = d4.at[4]
     for p in range(4):
-        c2t[p] = lax.dot_general(
-            l4[...], k2t[p], (((0,), (0,)), ((), ())), preferred_element_type=F32
-        ).astype(BF16)
-    bias4 = split_product(b2[...].reshape(1, 320), l4[...])
-    bias8 = split_product(bh[...].reshape(1, 640), l8[...])
-    y_up, y_down = pass_on(y_first, 4 + y, [y_ahead, y_behind])
-    a_copies = [copies.start(aa.at[(tc + o) % 8], at.at[tc], across[o]) for o in range(8)]
+        cols = pl.ds(2560 + 256 * p, 256)
+        pre = mm(xe[...], w[:, cols]) + bias8
+        unit, size = normed(pre)
+        unit_l[p // 2, p % 2] = unit[:OWN]
+        scale_l[p // 2, p % 2] = size[:OWN]
+        lat[p // 2 + 1, p % 2 + 1] = ((unit * gains[1, 0:1] + offsets[1, 0:1]) * keep).astype(BF16)
+
+    pyramid_level(
+        2, lat, back, unit_l, scale_l, conv.at[1], cot8, ring8, res8, gains[1], offsets[1], keep, shifts, split8, done8,
+        lambda: second_hop(1),
+    )
+
     for copy in small_copies:
         copy.wait_recv()
     sums = small_conv(laterals, small_h, mm, lambda t: t)
@@ -444,54 +501,13 @@
     grads = jnp.concatenate(grads)
     back_copies = exchange(grads, back_s, back_h)
 
-    z_ring = [(z - turn + 4) % 4, (z + turn + 4) % 4, (z + 2) % 4]
-    y_ring = [4 + (y - turn + 4) % 4, 4 + (y + turn + 4) % 4, 4 + (y + 2) % 4]
-    (z_on,) = pass_on(z_up, z_ring[0], [z_ahead])
-    (y_on,) = pass_on(y_up, y_ring[0], [y_ahead])
-    pass_on(z_down, z_ring[1], [])
-    pass_on(y_down, y_ring[1], [])
-
-    for copy in a_copies:
-        copy.wait_recv()
-    tile = at[...].reshape(OWN, 1280)
-    row = lax.broadcasted_iota(jnp.int32, (1280, 256), 0)
-    column = lax.broadcasted_iota(jnp.int32, (1280, 256), 1)
-    row = jnp.where(column % 16 < 10, row - column // 16 * 80 - column % 16, -1)
-
-    @pl.loop(0, 8)
-    def attn_columns(j):
-        attn_c[j] = mm(tile, (row == 10 * j).astype(F32).astype(BF16)).astype(BF16)
-
+    third_hop(1)
+    for copy in shared[1]:
+        copy.wait_recv()
     attn_copies = [
-        copies.start(attn_c.at[(tc + o) % 8], attn_h.at[tc], along[o - 1]) for o in range(1, 8)
+        copies.start(attn_c.at[(tc + o) % 8], attn_h.at[pl.ds(0, 8), tc], across[o]) for o in range(8)
     ]
-    attn_h[tc] = attn_c[tc]
-
-    for copy in back_copies:
-        copy.wait_recv()
-    sums = small_conv(grads, back_h, mt, lambda t: 8 - t)
-    steps = []
-    for i, weight in enumerate((l16, lc)):
-        unit, scale = units[i]
-        steps.append(mt(norm_back(unit, scale, sums[i] * gains[2 + i, 0:1]).astype(BF16), weight[...]))
-    hits = [jnp.where(q.astype(F32) == coarse.astype(F32), 1.0, 0.0) for q in quads]
-    portion = steps[1] / (hits[0] + hits[1] + hits[2] + hits[3])
-    total = steps[0]
-    for q in range(4):
-        total = total + mm(quad_t[q], (hits[q] * portion).astype(BF16))
-    dx_small[...] = total
-
-    for copy in halo_copies + cot_copies:
-        copy.wait_recv()
-    xe[:OWN] = x
-    xe[OWN:] = pick(ring_sel[...], xh[...].reshape(128, 1280))
-    ring4[...] = pick(cot_ring4[...], cot_h[...]).reshape(4, 4, RING, 256)
-    ring8[...] = pick(cot_ring8[...], cot_h[...]).reshape(2, 2, RING, 256)
-    pass_on(z_on, z_ring[2], [])
-    pass_on(y_on, y_ring[2], [])
-    for copy in shared:
-        copy.wait_recv()
-    keep = exists_mask(TOK, RING_SPANS)
+
     bias1, gain_m, shift_m = (ref[...].reshape(1, 640) for ref in (bias1, gain_m, shift_m))
     for p in range(4):
         cols = pl.ds(640 * p, 640)
@@ -504,6 +520,20 @@
         unit_u[p] = unit[:OWN]
         scale_u[p] = size[:OWN]
         slope_u[p] = (cdf[:OWN] + inner * jnp.exp(-0.5 * inner * inner) * (1 / np.sqrt(2 * np.pi))) * gain_m
+    for copy in back_copies:
+        copy.wait_recv()
+    sums = small_conv(grads, back_h, mt, lambda t: 8 - t)
+    steps = []
+    for i, weight in enumerate((l16, lc)):
+        unit, scale = units[i]
+        steps.append(mt(norm_back(unit, scale, sums[i] * gains[2 + i, 0:1]).astype(BF16), weight[...]))
+    hits = [jnp.where(q.astype(F32) == coarse.astype(F32), 1.0, 0.0) for q in quads]
+    portion = steps[1] / (hits[0] + hits[1] + hits[2] + hits[3])
+    total = steps[0]
+    for q in range(4):
+        total = total + mm(quad_t[q], (hits[q] * portion).astype(BF16))
+    dx_small[...] = total
+
     for p in range(4):
         for q in range(4):
             ph, pw = 2 * (p // 2) + q // 2, 2 * (p % 2) + q % 2
@@ -515,23 +545,8 @@
     def done4(ph, pw, grads):
         d4[2 * (ph // 2) + pw // 2, 2 * (ph % 2) + pw % 2] = grads
 
-    def done8(ph, pw, grads):
-        d8[2 * ph + pw] = grads
-
-    d8 = d4.at[4]
     pyramid_level(
-        4, lat, back, unit_l, scale_l, conv.at[0], cot4, ring4, out4, gains[0], offsets[0], keep, shifts, split4, done4
-    )
-    for p in range(4):
-        cols = pl.ds(2560 + 256 * p, 256)
-        pre = mm(xe[...], w[:, cols]) + bias8
-        unit, size = normed(pre)
-        unit_l[p // 2, p % 2] = unit[:OWN]
-        scale_l[p // 2, p % 2] = size[:OWN]
-        lat[p // 2 + 1, p % 2 + 1] = ((unit * gains[1, 0:1] + offsets[1, 0:1]) * keep).astype(BF16)
-
-    pyramid_level(
-        2, lat, back, unit_l, scale_l, conv.at[1], cot8, ring8, out8, gains[1], offsets[1], keep, shifts, split8, done8
+        4, lat, back, unit_l, scale_l, conv.at[0], cot4, ring4, res4, gains[0], offsets[0], keep, shifts, split4, done4
     )
     dup = jnp.zeros((4 * OWN, 640), F32)
     for q in range(4):
@@ -549,7 +564,7 @@
         twins[h].append(copies.start(block, block, sibling))
         return [copies.start(block, block, peer) for peer in peers]
 
-    rings, homes = [], []
+    rings = []
     for h in range(2):
         cols = pl.ds(640 * h, 640)
         grads = (mt(dfull[...], w[cols]) + dx_small[:, cols]).astype(BF16).reshape(8, 16, 640)
@@ -557,16 +572,20 @@
         block = tiles.at[h, tc]
         rings.append([copies.start(mine.at[h], block, peer) for peer in (z_ahead, z_behind)])
         twins[h].append(copies.start(mine.at[h], block, sibling))
-        homes += [copies.start(mine.at[h, (tc + o) % 8], home.at[h, tc], across[o]) for o in range(8)]
         tiles[h, tc] = grads
+    homes = [
+        copies.start(mine.at[h, (tc + o) % 8], home.at[h, tc], across[o]) for h in range(2) for o in range(8)
+    ]
     for copy in attn_copies:
         copy.wait_recv()
     for j in range(8):
-        attn_t[:, 128 * j : 128 * j + 128] = attn_h[j].T
+        attn_t[:, 128 * j : 128 * j + 128] = attn_h[j].reshape(OWN, 256).T
     onward = []
     for h in range(2):
         rings[h][0].wait_recv()
         onward += forward_tile(h, block_at[1], [z_ahead])
+    join_level(4, res4, out4, split4)
+    join_level(2, res8, out8, split8)
     sums = []
     for h in range(2):
         rings[h][1].wait_recv()
@@ -635,12 +654,26 @@
                 padded[i, j] = mm(shifts[3 * dy + dx + 4], source).astype(BF16)
 
 
-def pyramid_level(n, lat, back, unit, scale, conv, cot, ring, out, gains, offsets, keep, shifts, split, done):
+def join_level(n, res, out, split):
+    groups = n * n // 8 if n == 4 else 1
+    rows, tokens = ROWS // groups, 256 // n
+
+    @pl.loop(0, n)
+    def join(ph):
+        for g in range(groups):
+            block = jnp.concatenate([res[ph, pw, g * tokens : g * tokens + tokens] for pw in range(n)], axis=0)
+            block = mm(split[0], block).astype(BF16)
+            out[pl.ds(rows * g, rows), ph] = block.reshape(rows, 8 * n, 256)
+
+
+def pyramid_level(
+    n, lat, back, unit, scale, conv, cot, ring, res, gains, offsets, keep, shifts, split, done, between=None
+):
     groups = n * n // 8 if n == 4 else 1
     rows = ROWS // groups
     fill_shifted(lat, n, shifts)
 
-    @pl.loop(0, n)
+    @pl.loop(0, n, unroll=True)
     def forward(ph):
         acc = jnp.zeros((n * TOK, 256), F32)
         for t in range(9):
@@ -652,22 +685,19 @@
             block = cot[pl.ds(rows * g, rows), ph].reshape(256, 256)
             pieces.append(mm(split[1], block))
         tokens = 256 // n
-        results = []
         for pw in range(n):
             values, size = normed(acc[pw * TOK : pw * TOK + TOK])
-            results.append((values[:OWN] * gains[1:2] + offsets[1:2]).astype(BF16))
+            res[ph, pw] = (values[:OWN] * gains[1:2] + offsets[1:2]).astype(BF16)
             own = [piece[pw * tokens : pw * tokens + tokens] for piece in pieces]
             grads = jnp.concatenate(own + [ring[ph, pw].astype(F32)], axis=0)
             grads = norm_back(values, size, grads * gains[1:2])
             back[ph + 1, pw + 1] = (grads * keep).astype(BF16)
-        for g in range(groups):
-            block = jnp.concatenate([r[g * tokens : g * tokens + tokens] for r in results], axis=0)
-            block = mm(split[0], block).astype(BF16)
-            out[pl.ds(rows * g, rows), ph] = block.reshape(rows, 8 * n, 256)
-
+
+    if between is not None:
+        between()
     fill_shifted(back, n, shifts)
 
-    @pl.loop(0, n)
+    @pl.loop(0, n, unroll=True)
     def backward(ph):
         acc = jnp.zeros((n * OWN, 256), F32)
         for t in range(9):
@@ -685,7 +715,7 @@
 
     vmem, anywhere = pl.BlockSpec(memory_space=pltpu.VMEM), pl.BlockSpec(memory_space=pl.ANY)
     specs = [anywhere if i in (2, 3) else vmem for i in range(len(args))]
-    copies = 8 + 4 + 8 + 8 + 8 + 8 + 8 + 8 + 4 + 16 + 3 + 7 + 2 * (2 + 1 + 8 + 1 + 3 + 15)
+    copies = 8 + 4 + 8 + 8 + 8 + 8 + 8 + 8 + 4 + 16 + 3 + 2 * (2 + 1 + 8 + 1 + 3 + 15)
     return call(
         main_kernel,
         [
@@ -693,19 +723,20 @@
             shape((2, 8, 16, 640)), shape((2, 16, 16, 640)),
         ],
         [
-            buffer(1280, 3584), buffer(5, 80, 2, 2, 640), buffer(5, 80, 2, 2, 640),
-            buffer(8, 16, 1280), buffer(8, 16, 1280), buffer(8, 16, 1280), buffer(8, 16, 1280),
+            buffer(1280, 3584), buffer(4, 80, 2, 2, 640), buffer(4, 80, 2, 2, 640),
+            buffer(8, 16, 1280), buffer(8, 16, 1280), buffer(8, 16, 1280),
             buffer(8, 16, 1280), buffer(2, 16, 1280),
             buffer(SMALL, 256), buffer(SMALL, 256), buffer(SMALL, 256), buffer(SMALL, 256),
-            buffer(COT, 256), buffer(COT, 256), buffer(8, OWN, 256), buffer(8, OWN, 256),
+            buffer(COT, 256), buffer(COT, 256), buffer(8, 8, 16, 256), buffer(8, 8, 16, 256),
             buffer(TOK, 1280), buffer(4, 256, 640), buffer(4, 4, RING, 256), buffer(2, 2, RING, 256),
             wide(OWN, 1280), buffer(4, TOK, 640), wide(4, OWN, 640), wide(4, OWN, 640), wide(4, OWN, 1),
             buffer(6, 6, TOK, 256), buffer(6, 6, TOK, 256), wide(4, 4, OWN, 256), wide(4, 4, OWN, 1),
-            buffer(5, 4, OWN, 256), buffer(OWN, 3584), buffer(256, 1024),
+            buffer(5, 4, OWN, 256), buffer(OWN, 3584), buffer(4, 4, OWN, 256), buffer(2, 2, OWN, 256),
+            buffer(256, 1024),
             buffer(2, 8, 16, 640), buffer(2, 8, 16, 640), buffer(2, 8, 8, 16, 640),
             buffer(2, 16, 16, 640), buffer(2, 16, 16, 640),
             pltpu.SemaphoreType.DMA((copies,)), pltpu.SemaphoreType.DMA((copies,)),
-            pltpu.SemaphoreType.DMA((2, 5)),
+            pltpu.SemaphoreType.DMA((2, 4)),
         ],
         args,
         collective_id=0,

time: 108 us -> 102 us (0.944)
  Pallas kernels: 107 us -> 101 us
    pallas_call x2, Pallas kernels: 107 us -> 101 us  [call(): pl.pallas_call(kernel, out_shape=outs, in_specs=specs or [vmem] * len(arg...]
where the time goes in v3:
time: 102 us
  Pallas kernels  101 us (99%)
    pallas_call x2, Pallas kernels, call(): pl.pallas_call(kernel, out_shape=outs, in_specs=specs or [vmem] * len(arg...  101 us

profile of v3, /device:TPU:1, one launch (start us, length us, event | category | flops | bytes accessed | tf_op | source)
XLA Modules:
  0.0 101.8 jit_solution(2663802697634902359)
XLA Ops:
  0.6 98.3 %shard_map.361 = (bf16[16,4,32,256]{3,2,1,0:T(8,128)(2,1)}, bf16[16,2,16,256]{3,2,1,0:T(8,128)(2,1)}, bf16[16,8,256]{2,1,0:T(8,128)(2,1)}, bf16[8,4,256]{2,1,0:T...) custom-call(bf16[128,1280]{1,0:T(8,128)(2,1)} %bitcast.18, bf16[128,1280]{1,0:T(8,128)(2,1)} %bitcast.19, ...), custom_call_target="tpu_custom_call" | custom-call | tf_op jit(solution)/shard_map/pallas_call | solution.py:621
  99.0 2.9 %shard_map.362 = (bf16[128,1280]{1,0:T(8,128)(2,1)}, f32[10,1280]{1,0:T(8,128)}, bf16[16,4,32,256]{3,2,1,0:T(8,128)(2,1)}, bf16[16,2,16,256]{3,2,1,0:T(8,128)(2,...) custom-call(bf16[2,8,16,640]{3,2,1,0:T(8,128)(2,1)} %get-tuple-element.18.home, ...), custom_call_target="tpu_custom_call" | custom-call | tf_op jit(solution)/shard_map/pallas_call | solution.py:621
